TPU v7x, 128 devices: a whole 4x4x4 slice. The times are simulated.
128 devices in a mesh: tm: 8 (over y_lo, x), space: 16 (over y_hi, z, core).
Axes of the slice: x: 4, y: 4 (y_hi: 2, y_lo: 2; y = y_hi * 2 + y_lo), z: 4, core: 2. Of those that a mesh axis runs over, the one named last changes fastest.
Arguments:
- query_time: bfloat16 [64, 1024, 1152], P('tm', 'space'), may hold values from -6 to 6
- key_time: bfloat16 [64, 1024, 1152], P('tm', 'space'), may hold values from -6 to 6
- value_time: bfloat16 [64, 1024, 1152], P('tm', 'space'), may hold values from -6 to 6
- query_space: bfloat16 [64, 1024, 1152], P('tm', 'space'), may hold values from -6 to 6
- key_space: bfloat16 [64, 1024, 1152], P('tm', 'space'), may hold values from -6 to 6
- value_space: bfloat16 [64, 1024, 1152], P('tm', 'space'), may hold values from -6 to 6
- grad_output: bfloat16 [64, 1024, 1152], P('tm', 'space'), may hold values from -6 to 6
- outproj_time: bfloat16 [1152, 1152], replicated, may hold values from -0.1875 to 0.1875
- queryproj_time: bfloat16 [1152, 1152], replicated, may hold values from -0.1875 to 0.1875
- keyproj_time: bfloat16 [1152, 1152], replicated, may hold values from -0.1875 to 0.1875
- valueproj_time: bfloat16 [1152, 1152], replicated, may hold values from -0.1875 to 0.1875
- outproj_space: bfloat16 [1152, 1152], replicated, may hold values from -0.1875 to 0.1875
Outputs:
- query_grad: bfloat16 [64, 1024, 1152], P('tm', 'space')
- key_grad: bfloat16 [64, 1024, 1152], P('tm', 'space')
- value_grad: bfloat16 [64, 1024, 1152], P('tm', 'space')
- middle_grad: bfloat16 [64, 1024, 1152], P('tm', 'space')
All inputs are finite; a program needn't handle non-finite values.
Results may differ from a plain program's by a relative error of at most 0.03.
Values may be sent and summed in bfloat16 or wider, within the bound.
No kernel may reach another device: no remote copies, remote signals or barrier semaphores. Data moves between devices by JAX's collectives and lax.ppermute only.
A program may use at most 128 MiB of HBM per device.

v0:
```python
import jax
import jax.numpy as jnp
from jax import lax
from jax.sharding import PartitionSpec as P

HEAD_DIM = 72


def back_project(rows, weight):
    return lax.dot_general(
        rows, weight, (((rows.ndim - 1,), (1,)), ((), ())), preferred_element_type=jnp.float32
    )


def attend_back(query, keys, values, grad, layout):
    leading = query.shape[:-1]
    head_count = query.shape[-1] // HEAD_DIM
    query, keys, values, grad = [
        member.reshape(leading + (head_count, HEAD_DIM)) for member in (query, keys, values, grad)
    ]
    partner = layout.replace("l", "m")
    factor = HEAD_DIM ** (-0.5)
    scores = (
        jnp.einsum(
            layout + "," + partner + "->bhlm", query, keys, preferred_element_type=jnp.float32
        )
        * factor
    )
    weights = jax.nn.softmax(scores, axis=-1)
    weights_half = weights.astype(jnp.bfloat16)
    grad_weights = jnp.einsum(
        layout + "," + partner + "->bhlm", grad, values, preferred_element_type=jnp.float32
    )
    centre = jnp.sum(weights * grad_weights, axis=-1, keepdims=True)
    grad_scores = (weights * (grad_weights - centre)).astype(jnp.bfloat16)
    query_grad = (
        jnp.einsum(
            "bhlm," + partner + "->" + layout, grad_scores, keys, preferred_element_type=jnp.float32
        )
        * factor
    ).astype(jnp.bfloat16)
    key_grad = (
        jnp.einsum(
            "bhlm," + layout + "->" + partner,
            grad_scores,
            query,
            preferred_element_type=jnp.float32,
        )
        * factor
    ).astype(jnp.bfloat16)
    value_grad = jnp.einsum(
        "bhlm," + layout + "->" + partner, weights_half, grad, preferred_element_type=jnp.float32
    ).astype(jnp.bfloat16)
    return tuple(
        (
            member.reshape(leading + (head_count * HEAD_DIM,))
            for member in (query_grad, key_grad, value_grad)
        )
    )


def spatial_core(query, keys, values, grad):
    frame_count = query.shape[0]
    group = 2
    rest = query.shape[1:]

    def grouped(member):
        return member.reshape((frame_count // group, group) + rest)

    def frame_group(members):
        return attend_back(members[0], members[1], members[2], members[3], "blhe")

    result = lax.map(frame_group, (grouped(query), grouped(keys), grouped(values), grouped(grad)))
    return tuple((member.reshape((frame_count,) + rest) for member in result))


def per_device(
    query_time,
    key_time,
    value_time,
    query_space,
    key_space,
    value_space,
    grad_output,
    outproj_time,
    queryproj_time,
    keyproj_time,
    valueproj_time,
    outproj_space,
):
    grad_time = back_project(grad_output, outproj_time).astype(jnp.bfloat16)
    pieces = (
        lax.all_to_all(query_time, "tm", split_axis=2, concat_axis=0, tiled=True),
        lax.all_to_all(key_time, "tm", split_axis=2, concat_axis=0, tiled=True),
        lax.all_to_all(value_time, "tm", split_axis=2, concat_axis=0, tiled=True),
        lax.all_to_all(grad_time, "tm", split_axis=2, concat_axis=0, tiled=True),
    )
    result = attend_back(pieces[0], pieces[1], pieces[2], pieces[3], "lbhe")
    middle = (
        grad_output.astype(jnp.float32)
        + back_project(
            lax.all_to_all(result[0], "tm", split_axis=0, concat_axis=2, tiled=True), queryproj_time
        )
        + back_project(
            lax.all_to_all(result[1], "tm", split_axis=0, concat_axis=2, tiled=True), keyproj_time
        )
        + back_project(
            lax.all_to_all(result[2], "tm", split_axis=0, concat_axis=2, tiled=True), valueproj_time
        )
    )
    middle_grad = middle.astype(jnp.bfloat16)
    grad_space = back_project(middle_grad, outproj_space).astype(jnp.bfloat16)
    pieces = (
        lax.all_to_all(query_space, "space", split_axis=2, concat_axis=1, tiled=True),
        lax.all_to_all(key_space, "space", split_axis=2, concat_axis=1, tiled=True),
        lax.all_to_all(value_space, "space", split_axis=2, concat_axis=1, tiled=True),
        lax.all_to_all(grad_space, "space", split_axis=2, concat_axis=1, tiled=True),
    )
    result = spatial_core(pieces[0], pieces[1], pieces[2], pieces[3])
    return (
        lax.all_to_all(result[0], "space", split_axis=1, concat_axis=2, tiled=True),
        lax.all_to_all(result[1], "space", split_axis=1, concat_axis=2, tiled=True),
        lax.all_to_all(result[2], "space", split_axis=1, concat_axis=2, tiled=True),
        middle_grad,
    )


def solution(mesh):
    in_specs = (
        P("tm", "space", None),
        P("tm", "space", None),
        P("tm", "space", None),
        P("tm", "space", None),
        P("tm", "space", None),
        P("tm", "space", None),
        P("tm", "space", None),
        P(),
        P(),
        P(),
        P(),
        P(),
    )
    out_specs = (
        P("tm", "space", None),
        P("tm", "space", None),
        P("tm", "space", None),
        P("tm", "space", None),
    )
    return jax.shard_map(
        per_device, mesh=mesh, in_specs=in_specs, out_specs=out_specs, check_vma=False
    )
```

profile of v0, /device:TPU:111, one launch (start us, length us, event | category | flops | bytes accessed | tf_op | source)
XLA Modules:
  0.0 579.9 jit_solution(4013073059068543045)
XLA Ops:
  4.9 4.5 reshape.168
  9.4 5.1 all-to-all-start.2
  18.5 4.5 reshape.166
  23.0 5.5 all-to-all-done.2
  28.6 7.4 %all-to-all-start.3 = ((bf16[8,2,36864]{2,1,0:T(2,128)(2,1)}), bf16[8,2,36864]{2,1,0:T(2,128)(2,1)}, u32[]{:S(2)}, u32[]{:S(2)}) async-start(bf16[8,2,36864]{2,1,0:T(2,128)(2,1)} %reshape.166), calls=%async_computation.3 | async-start | bytes 2359296 | tf_op jit(solution)/shard_map/all_to_all | solution.py:94
  50.1 7.4 %all-to-all-start.4 = ((bf16[8,2,36864]{2,1,0:T(2,128)(2,1)}), bf16[8,2,36864]{2,1,0:T(2,128)(2,1)}, u32[]{:S(2)}, u32[]{:S(2)}) async-start(bf16[8,2,36864]{2,1,0:T(2,128)(2,1)} %reshape.164), calls=%async_computation.4 | async-start | bytes 2359296 | tf_op jit(solution)/shard_map/all_to_all | solution.py:96
  63.3 8.3 %all-to-all-done.4 = bf16[8,2,36864]{2,1,0:T(2,128)(2,1)} async-done(((bf16[8,2,36864]{2,1,0:T(2,128)(2,1)}), bf16[8,2,36864]{2,1,0:T(2,128)(2,1)}, u32[]{:S(2)}, u32[]{:S(2)}) %all-to-all-start.4) | async-done | bytes 1179680 | tf_op jit(solution)/shard_map/all_to_all | solution.py:96
  71.6 7.4 %all-to-all-start.5 = ((bf16[8,2,36864]{2,1,0:T(2,128)(2,1)}), bf16[8,2,36864]{2,1,0:T(2,128)(2,1)}, u32[]{:S(2)}, u32[]{:S(2)}) async-start(bf16[8,2,36864]{2,1,0:T(2,128)(2,1)} %reshape.162), calls=%async_computation.5 | async-start | bytes 2359296 | tf_op jit(solution)/shard_map/all_to_all | solution.py:95
  109.4 4.7 reshape.165
  114.1 4.5 copy.91
  122.9 7.7 %all-to-all-start = ((bf16[16,2,18432]{2,1,0:T(2,128)(2,1)}), bf16[16,2,18432]{2,1,0:T(2,128)(2,1)}, u32[]{:S(2)}, u32[]{:S(2)}) async-start(bf16[16,2,18432]{2,1,0:T(2,128)(2,1)} %reshape.158), calls=%async_computation | async-start | bytes 2359296 | tf_op jit(solution)/shard_map/all_to_all | solution.py:115
  130.6 4.4 reshape.163
  135.0 4.5 copy.93
  147.9 6.2 %fusion.103 = (f32[64,2,64]{2,1,0:T(2,128)S(1)}, f32[64,2,64,64]{2,3,1,0:T(8,128)S(1)}) fusion(f32[64,2,64,64]{2,3,1,0:T(8,128)S(1)} %fusion.83), kind=kOutput, calls=%fused_computation.90 | output fusion | flops 2097215 | bytes 4227072 | tf_op jit(solution)/shard_map/sub | solution.py:29
  156.1 5.4 multiply_reduce_fusion.2
  161.5 7.6 %all-to-all-start.1 = ((bf16[16,2,18432]{2,1,0:T(2,128)(2,1)}), bf16[16,2,18432]{2,1,0:T(2,128)(2,1)}, u32[]{:S(2)}, u32[]{:S(2)}) async-start(bf16[16,2,18432]{2,1,0:T(2,128)(2,1)} %reshape.160), calls=%async_computation.1 | async-start | bytes 2359296 | tf_op jit(solution)/shard_map/all_to_all | solution.py:114
  169.1 4.9 multiply_convert_fusion.3
  187.1 5.1 all-to-all-start.7
  201.0 20.6 %all-to-all-done.7 = bf16[64,64,144]{2,1,0:T(8,128)(2,1)} async-done(((bf16[64,64,144]{2,1,0:T(8,128)(2,1)}), bf16[64,64,144]{2,1,0:T(8,128)(2,1)}, u32[]{:S(2)}, u32[]{:S(2)}) %all-to-all-start.7) | async-done | bytes 1179680 | tf_op jit(solution)/shard_map/all_to_all | solution.py:105
  221.6 5.1 all-to-all-start.6
  226.7 4.9 convert_bitcast_fusion
  239.5 11.0 %all-to-all-done.6 = bf16[64,64,144]{2,1,0:T(8,128)(2,1)S(1)} async-done(((bf16[64,64,144]{2,1,0:T(8,128)(2,1)}), bf16[64,64,144]{2,1,0:T(8,128)(2,1)S(1)}, u32[]{:S(2)}, u32[]{:S(2)}) %all-to-all-start.6) | async-done | bytes 1179680 | tf_op jit(solution)/shard_map/all_to_all | solution.py:102
  251.8 7.5 %all-to-all-start.8 = ((bf16[64,64,144]{2,1,0:T(8,128)(2,1)}), bf16[64,64,144]{2,1,0:T(8,128)(2,1)}, u32[]{:S(2)}, u32[]{:S(2)}) async-start(bf16[64,64,144]{2,1,0:T(8,128)(2,1)} %reshape.147), calls=%async_computation.8 | async-start | bytes 4194304 | tf_op jit(solution)/shard_map/all_to_all | solution.py:108
  269.0 4.6 all_to_all.191
  279.9 5.0 convolution_add_fusion.2
  286.8 6.5 %all-to-all-start.10 = ((bf16[16,2,18432]{2,1,0:T(2,128)(2,1)}), bf16[16,2,18432]{2,1,0:T(2,128)(2,1)}, u32[]{:S(2)}, u32[]{:S(2)}) async-start(bf16[16,2,18432]{2,1,0:T(2,128)(2,1)} %reshape.172), calls=%async_computation.10 | async-start | bytes 2359296 | tf_op jit(solution)/shard_map/all_to_all | solution.py:116
  293.3 5.7 convolution_add_fusion.1
  304.8 4.8 fusion.67
  319.0 7.6 %all-to-all-start.9 = ((bf16[16,2,18432]{2,1,0:T(2,128)(2,1)}), bf16[16,2,18432]{2,1,0:T(2,128)(2,1)}, u32[]{:S(2)}, u32[]{:S(2)}) async-start(bf16[16,2,18432]{2,1,0:T(2,128)(2,1)} %reshape.170), calls=%async_computation.9 | async-start | bytes 2359296 | tf_op jit(solution)/shard_map/all_to_all | solution.py:117
  371.8 82.5 %while.14 = (s32[]{:T(128)}, bf16[4,2,1024,72]{2,3,1,0:T(8,128)(2,1)}, bf16[4,2,1024,72]{2,3,1,0:T(8,128)(2,1)}, bf16[4,2,1024,72]{2,3,1,0:T(8,128)(2,1)}, bf16[...) while((s32[]{:T(128)}, ...), condition=%wide.region_7.8_spmd, body=%wide.region_3.7_spmd.sunk | while | flops 1535851520 | bytes 100521160 | solution.py:73
  371.8 5.0 fusion.133
  376.9 5.0 multiply_reduce_fusion.5
  392.5 5.0 fusion.133
  397.5 5.0 multiply_reduce_fusion.5
  413.1 5.0 fusion.133
  418.1 5.0 multiply_reduce_fusion.5
  433.7 5.0 fusion.133
  438.8 5.0 multiply_reduce_fusion.5
  454.4 6.0 %copy.110 = bf16[4,2,1024,72]{3,1,0,2:T(2,128)(2,1)} copy(bf16[4,2,1024,72]{2,3,1,0:T(8,128)(2,1)} %get-tuple-element.48) | data formatting | bytes 2359296 | tf_op jit(solution)/shard_map/while | solution.py:73
  460.3 7.2 %all-to-all-start.11 = ((bf16[8,1024,72]{2,0,1:T(8,128)(2,1)}), bf16[8,1024,72]{2,0,1:T(8,128)(2,1)S(1)}, u32[]{:S(2)}, u32[]{:S(2)}) async-start(bf16[8,1024,72]{2,0,1:T(8,128)(2,1)} %bitcast.244), calls=%async_computation.11 | async-start | bytes 4194304 | tf_op jit(solution)/shard_map/all_to_all | solution.py:121
  467.6 6.0 %copy.113 = bf16[4,2,1024,72]{3,1,0,2:T(2,128)(2,1)} copy(bf16[4,2,1024,72]{2,3,1,0:T(8,128)(2,1)} %get-tuple-element.49) | data formatting | bytes 2359296 | tf_op jit(solution)/shard_map/while | solution.py:73
  473.6 25.2 %all-to-all-done.11 = bf16[8,1024,72]{2,0,1:T(8,128)(2,1)S(1)} async-done(((bf16[8,1024,72]{2,0,1:T(8,128)(2,1)}), bf16[8,1024,72]{2,0,1:T(8,128)(2,1)S(1)}, u32[]{:S(2)}, u32[]{:S(2)}) %all-to-all-start.11) | async-done | bytes 1179680 | tf_op jit(solution)/shard_map/all_to_all | solution.py:121
  503.2 6.0 %copy.116 = bf16[4,2,1024,72]{3,1,0,2:T(2,128)(2,1)} copy(bf16[4,2,1024,72]{2,3,1,0:T(8,128)(2,1)} %get-tuple-element.50) | data formatting | bytes 2359296 | tf_op jit(solution)/shard_map/while | solution.py:73
  509.2 25.3 %all-to-all-done.12 = bf16[8,1024,72]{2,0,1:T(8,128)(2,1)} async-done(((bf16[8,1024,72]{2,0,1:T(8,128)(2,1)}), bf16[8,1024,72]{2,0,1:T(8,128)(2,1)}, u32[]{:S(2)}, u32[]{:S(2)}) %all-to-all-start.12) | async-done | bytes 1179680 | tf_op jit(solution)/shard_map/all_to_all | solution.py:122
  534.5 4.8 all-to-all-start.13
  542.0 4.6 all_to_all.205
  553.0 17.5 %all-to-all-done.13 = bf16[8,1024,72]{2,0,1:T(8,128)(2,1)} async-done(((bf16[8,1024,72]{2,0,1:T(8,128)(2,1)}), bf16[8,1024,72]{2,0,1:T(8,128)(2,1)}, u32[]{:S(2)}, u32[]{:S(2)}) %all-to-all-start.13) | async-done | bytes 1179680 | tf_op jit(solution)/shard_map/all_to_all | solution.py:123
  574.9 4.6 all_to_all.213
  (147 shorter events, 242.6 us)
Async XLA Ops:
  0.6 35.3 %copy-start = (bf16[1152,1152]{1,0:T(8,128)(2,1)S(1)}, bf16[1152,1152]{1,0:T(8,128)(2,1)}, u32[]{:S(2)}) copy-start(bf16[1152,1152]{1,0:T(8,128)(2,1)} %param.21) | copy-start | bytes 7962628
  9.4 19.2 %all-to-all-start.2 = ((bf16[8,2,36864]{2,1,0:T(2,128)(2,1)}), bf16[8,2,36864]{2,1,0:T(2,128)(2,1)}, u32[]{:S(2)}, u32[]{:S(2)}) async-start(bf16[8,2,36864]{2,1,0:T(2,128)(2,1)} %reshape.168), calls=%async_computation.2 | async-start | bytes 2359296 | tf_op jit(solution)/shard_map/all_to_all | solution.py:93
  28.6 21.5 %all-to-all-start.3 = ((bf16[8,2,36864]{2,1,0:T(2,128)(2,1)}), bf16[8,2,36864]{2,1,0:T(2,128)(2,1)}, u32[]{:S(2)}, u32[]{:S(2)}) async-start(bf16[8,2,36864]{2,1,0:T(2,128)(2,1)} %reshape.166), calls=%async_computation.3 | async-start | bytes 2359296 | tf_op jit(solution)/shard_map/all_to_all | solution.py:94
  50.1 21.5 %all-to-all-start.4 = ((bf16[8,2,36864]{2,1,0:T(2,128)(2,1)}), bf16[8,2,36864]{2,1,0:T(2,128)(2,1)}, u32[]{:S(2)}, u32[]{:S(2)}) async-start(bf16[8,2,36864]{2,1,0:T(2,128)(2,1)} %reshape.164), calls=%async_computation.4 | async-start | bytes 2359296 | tf_op jit(solution)/shard_map/all_to_all | solution.py:96
  71.6 51.3 %all-to-all-start.5 = ((bf16[8,2,36864]{2,1,0:T(2,128)(2,1)}), bf16[8,2,36864]{2,1,0:T(2,128)(2,1)}, u32[]{:S(2)}, u32[]{:S(2)}) async-start(bf16[8,2,36864]{2,1,0:T(2,128)(2,1)} %reshape.162), calls=%async_computation.5 | async-start | bytes 2359296 | tf_op jit(solution)/shard_map/all_to_all | solution.py:95
  109.4 34.4 %copy-start.2 = (bf16[64,64,2,72]{3,2,1,0:T(2,128)(2,1)}, bf16[64,64,2,72]{3,2,1,0:T(2,128)(2,1)S(1)}, u32[]{:S(2)}) copy-start(bf16[64,64,2,72]{3,2,1,0:T(2,128)(2,1)S(1)} %reshape.142) | copy-start | bytes 3538948
  122.9 38.6 %all-to-all-start = ((bf16[16,2,18432]{2,1,0:T(2,128)(2,1)}), bf16[16,2,18432]{2,1,0:T(2,128)(2,1)}, u32[]{:S(2)}, u32[]{:S(2)}) async-start(bf16[16,2,18432]{2,1,0:T(2,128)(2,1)} %reshape.158), calls=%async_computation | async-start | bytes 2359296 | tf_op jit(solution)/shard_map/all_to_all | solution.py:115
  147.9 8.2 %copy-start.9 = (bf16[64,64,2,72]{3,2,1,0:T(2,128)(2,1)S(1)}, bf16[64,64,2,72]{3,2,1,0:T(2,128)(2,1)}, u32[]{:S(2)}) copy-start(bf16[64,64,2,72]{3,2,1,0:T(2,128)(2,1)} %reshape.143) | copy-start | bytes 3538948
  147.9 8.2 %copy-start.10 = (bf16[64,64,2,72]{3,2,1,0:T(2,128)(2,1)S(1)}, bf16[64,64,2,72]{3,2,1,0:T(2,128)(2,1)}, u32[]{:S(2)}) copy-start(bf16[64,64,2,72]{3,2,1,0:T(2,128)(2,1)} %reshape.144) | copy-start | bytes 3538948
  154.1 2.0 copy-start.4
  161.5 25.6 %all-to-all-start.1 = ((bf16[16,2,18432]{2,1,0:T(2,128)(2,1)}), bf16[16,2,18432]{2,1,0:T(2,128)(2,1)}, u32[]{:S(2)}, u32[]{:S(2)}) async-start(bf16[16,2,18432]{2,1,0:T(2,128)(2,1)} %reshape.160), calls=%async_computation.1 | async-start | bytes 2359296 | tf_op jit(solution)/shard_map/all_to_all | solution.py:114
  169.1 4.9 copy-start.3
  187.1 34.5 %all-to-all-start.7 = ((bf16[64,64,144]{2,1,0:T(8,128)(2,1)}), bf16[64,64,144]{2,1,0:T(8,128)(2,1)}, u32[]{:S(2)}, u32[]{:S(2)}) async-start(bf16[64,64,144]{2,1,0:T(8,128)(2,1)} %reshape.146), calls=%async_computation.7 | async-start | bytes 4194304 | tf_op jit(solution)/shard_map/all_to_all | solution.py:105
  221.6 28.9 %all-to-all-start.6 = ((bf16[64,64,144]{2,1,0:T(8,128)(2,1)}), bf16[64,64,144]{2,1,0:T(8,128)(2,1)S(1)}, u32[]{:S(2)}, u32[]{:S(2)}) async-start(bf16[64,64,144]{2,1,0:T(8,128)(2,1)} %reshape.145), calls=%async_computation.6 | async-start | bytes 4194304 | tf_op jit(solution)/shard_map/all_to_all | solution.py:102
  250.5 1.3 copy-start.5
  251.8 35.0 %all-to-all-start.8 = ((bf16[64,64,144]{2,1,0:T(8,128)(2,1)}), bf16[64,64,144]{2,1,0:T(8,128)(2,1)}, u32[]{:S(2)}, u32[]{:S(2)}) async-start(bf16[64,64,144]{2,1,0:T(8,128)(2,1)} %reshape.147), calls=%async_computation.8 | async-start | bytes 4194304 | tf_op jit(solution)/shard_map/all_to_all | solution.py:108
  269.0 4.6 copy-start.6
  276.2 3.8 copy-start.15
  285.0 8.3 %copy-start.13 = (bf16[8,64,1152]{2,1,0:T(8,128)(2,1)S(1)}, bf16[8,64,1152]{2,1,0:T(8,128)(2,1)}, u32[]{:S(2)}) copy-start(bf16[8,64,1152]{2,1,0:T(8,128)(2,1)} %all_to_all.191) | copy-start | bytes 3538948
  286.8 32.2 %all-to-all-start.10 = ((bf16[16,2,18432]{2,1,0:T(2,128)(2,1)}), bf16[16,2,18432]{2,1,0:T(2,128)(2,1)}, u32[]{:S(2)}, u32[]{:S(2)}) async-start(bf16[16,2,18432]{2,1,0:T(2,128)(2,1)} %reshape.172), calls=%async_computation.10 | async-start | bytes 2359296 | tf_op jit(solution)/shard_map/all_to_all | solution.py:116
  304.8 5.9 %copy-start.14 = (bf16[1152,1152]{1,0:T(8,128)(2,1)S(1)}, bf16[1152,1152]{1,0:T(8,128)(2,1)}, u32[]{:S(2)}) copy-start(bf16[1152,1152]{1,0:T(8,128)(2,1)} %param.25) | copy-start | bytes 7962628
  309.7 1.0 copy-start.16
  319.0 41.2 %all-to-all-start.9 = ((bf16[16,2,18432]{2,1,0:T(2,128)(2,1)}), bf16[16,2,18432]{2,1,0:T(2,128)(2,1)}, u32[]{:S(2)}, u32[]{:S(2)}) async-start(bf16[16,2,18432]{2,1,0:T(2,128)(2,1)} %reshape.170), calls=%async_computation.9 | async-start | bytes 2359296 | tf_op jit(solution)/shard_map/all_to_all | solution.py:117
  367.4 4.4 copy-start.7
  367.4 4.4 copy-start.8
  376.9 5.0 slice-start
  376.9 6.0 %slice-start.1 = ((s8[8388608]{0:T(1024)(128)(4,1)}), s8[4194304]{0:T(1024)(128)(4,1)S(1)}, s32[]{:S(2)}) async-start(s8[8388608]{0:T(1024)(128)(4,1)} %bitcast.218), calls=%async_computation.15 | async-start | bytes 8388608 | tf_op jit(solution)/shard_map/while
  385.3 2.1 copy-start.11
  388.4 1.0 copy-start.12
  397.5 5.0 slice-start
  397.5 6.0 %slice-start.1 = ((s8[8388608]{0:T(1024)(128)(4,1)}), s8[4194304]{0:T(1024)(128)(4,1)S(1)}, s32[]{:S(2)}) async-start(s8[8388608]{0:T(1024)(128)(4,1)} %bitcast.218), calls=%async_computation.15 | async-start | bytes 8388608 | tf_op jit(solution)/shard_map/while
  406.0 2.1 copy-start.11
  409.0 1.0 copy-start.12
  418.1 5.0 slice-start
  418.1 6.0 %slice-start.1 = ((s8[8388608]{0:T(1024)(128)(4,1)}), s8[4194304]{0:T(1024)(128)(4,1)S(1)}, s32[]{:S(2)}) async-start(s8[8388608]{0:T(1024)(128)(4,1)} %bitcast.218), calls=%async_computation.15 | async-start | bytes 8388608 | tf_op jit(solution)/shard_map/while
  426.6 2.1 copy-start.11
  429.6 1.0 copy-start.12
  438.8 5.0 slice-start
  438.8 6.0 %slice-start.1 = ((s8[8388608]{0:T(1024)(128)(4,1)}), s8[4194304]{0:T(1024)(128)(4,1)S(1)}, s32[]{:S(2)}) async-start(s8[8388608]{0:T(1024)(128)(4,1)} %bitcast.218), calls=%async_computation.15 | async-start | bytes 8388608 | tf_op jit(solution)/shard_map/while
  447.2 2.1 copy-start.11
  450.3 1.0 copy-start.12
  460.3 38.4 %all-to-all-start.11 = ((bf16[8,1024,72]{2,0,1:T(8,128)(2,1)}), bf16[8,1024,72]{2,0,1:T(8,128)(2,1)S(1)}, u32[]{:S(2)}, u32[]{:S(2)}) async-start(bf16[8,1024,72]{2,0,1:T(8,128)(2,1)} %bitcast.244), calls=%async_computation.11 | async-start | bytes 4194304 | tf_op jit(solution)/shard_map/all_to_all | solution.py:121
  498.8 35.7 %all-to-all-start.12 = ((bf16[8,1024,72]{2,0,1:T(8,128)(2,1)}), bf16[8,1024,72]{2,0,1:T(8,128)(2,1)}, u32[]{:S(2)}, u32[]{:S(2)}) async-start(bf16[8,1024,72]{2,0,1:T(8,128)(2,1)} %bitcast.243), calls=%async_computation.12 | async-start | bytes 4194304 | tf_op jit(solution)/shard_map/all_to_all | solution.py:122
  534.5 36.0 %all-to-all-start.13 = ((bf16[8,1024,72]{2,0,1:T(8,128)(2,1)}), bf16[8,1024,72]{2,0,1:T(8,128)(2,1)}, u32[]{:S(2)}, u32[]{:S(2)}) async-start(bf16[8,1024,72]{2,0,1:T(8,128)(2,1)} %bitcast.242), calls=%async_computation.13 | async-start | bytes 4194304 | tf_op jit(solution)/shard_map/all_to_all | solution.py:123
  570.5 9.0 %copy-start.1 = (bf16[1152,1152]{1,0:T(8,128)(2,1)S(1)}, bf16[1152,1152]{1,0:T(8,128)(2,1)}, u32[]{:S(2)}) copy-start(bf16[1152,1152]{1,0:T(8,128)(2,1)} %param.21) | copy-start | bytes 7962628
where the time goes:
time: 591 us; the launch traced here: 580 us
  local copies, waits for them, and re-layouts  236 us (40%)
  waiting for transfers between devices  122 us (21%)
  matrix products  108 us (18%)
  starting transfers between devices  90.8 us (15%)
  other arithmetic  20.8 us (4%)
    unnamed x52, local copies, waits for them, and re-layouts  80.8 us
    dot_general x5, matrix products, attend_back(): jnp.einsum(layout + ',' + partner + '->bhlm', grad, values, preferred_ele...  25.5 us
    all_to_all x1, waiting for transfers between devices, per_device(): lax.all_to_all(result[1], 'space', split_axis=1, concat_axis=2, tiled=True)  25.3 us
    all_to_all x1, waiting for transfers between devices, per_device(): lax.all_to_all(result[0], 'space', split_axis=1, concat_axis=2, tiled=True)  25.2 us
    dot_general x5, matrix products, back_project(): lax.dot_general(rows, weight, (((rows.ndim - 1,), (1,)), ((), ())), prefe...  22.7 us
    all_to_all x1, waiting for transfers between devices, per_device(): lax.all_to_all(result[1], 'tm', split_axis=0, concat_axis=2, tiled=True)  20.6 us
    sub x4, matrix products, attend_back(): weights = jax.nn.softmax(scores, axis=-1)  20.1 us
    while x3, local copies, waits for them, and re-layouts, spatial_core(): lax.map(frame_group, (grouped(query), grouped(keys), grouped(values), gro...  18 us
  transfers between devices with their start and end apart: 14, of which 10 were waited for; matrix products, arithmetic and copies ran while one was open for 39% of the time, Pallas kernels for 0%

commit v1 on v0

v1 whole, which is shorter than its diff:
```python
import jax
import jax.numpy as jnp
from jax import lax
from jax.experimental import pallas as pl
from jax.experimental.pallas import tpu as pltpu
from jax.sharding import PartitionSpec as P

HEAD_DIM = 72
D = 1152
HALF = 640
SCALE = HEAD_DIM**-0.5
LOG2E = 1.4426950408889634
BF = jnp.bfloat16
F32 = jnp.float32
VMEM_LIMIT = 56 * 1024 * 1024


def nn(a, b):
    return lax.dot_general(a, b, (((1,), (0,)), ((), ())), preferred_element_type=F32)


def nt(a, b):
    return lax.dot_general(a, b, (((1,), (1,)), ((), ())), preferred_element_type=F32)


def tn(a, b):
    return lax.dot_general(a, b, (((0,), (0,)), ((), ())), preferred_element_type=F32)


def lane_mask(rows, low):
    lane = lax.broadcasted_iota(jnp.int32, (rows, 256), 1)
    return (lane >= low) & (lane < low + HEAD_DIM)


def permutation(inner):
    outer = 512 // inner
    row = lax.broadcasted_iota(jnp.int32, (512, 512), 0)
    column = lax.broadcasted_iota(jnp.int32, (512, 512), 1)
    return (column == inner * (row % outer) + row // outer).astype(BF)


def temporal_kernel(
    r_ref, wo_hbm, wq_hbm, wk_hbm, wv_hbm, out_ref,
    wo, wq, wk, wv, q, k, v, g0, g, dq, dk, dv, sems,
):
    copies = [
        pltpu.make_async_copy(src, dst, sems.at[i])
        for i, (src, dst) in enumerate(((wo_hbm, wo), (wq_hbm, wq), (wk_hbm, wk), (wv_hbm, wv)))
    ]
    for copy in copies:
        copy.start()
    to_patch = permutation(8)
    for a, dst in enumerate((q, k, v, g0)):
        dst[...] = nn(to_patch, r_ref[:, a].reshape(512, D)).astype(BF)
    copies[0].wait()
    g[...] = nt(g0[...], wo[...]).astype(BF)
    m_patch = lax.broadcasted_iota(jnp.int32, (128, 128), 0) // 64
    l_patch = lax.broadcasted_iota(jnp.int32, (128, 128), 1) // 64
    same = m_patch == l_patch

    def head(h, carry):
        first = jnp.minimum(h * HEAD_DIM // 128, D // 128 - 2) * 128
        window = pl.ds(pl.multiple_of(first, 128), 256)
        mask = lane_mask(128, h * HEAD_DIM - first)
        for b in range(4):
            rows = pl.ds(b * 128, 128)
            qb, kb, vb, gb = [ref[rows, window] for ref in (q, k, v, g)]
            kh = jnp.where(mask, kb, jnp.zeros_like(kb))
            vh = jnp.where(mask, vb, jnp.zeros_like(vb))
            s = jnp.where(same, nt(kh, qb) * (SCALE * LOG2E), -1e30)
            p = jnp.exp2(s - jnp.max(s, axis=0, keepdims=True))
            p = p * (1.0 / jnp.sum(p, axis=0, keepdims=True))
            dp = nt(vh, gb)
            delta = jnp.sum(p * dp, axis=0, keepdims=True)
            ds = (p * (dp - delta)).astype(BF)
            new_dk = (nn(ds, qb) * SCALE).astype(BF)
            new_dv = nn(p.astype(BF), gb).astype(BF)
            new_dq = (tn(ds, kb) * SCALE).astype(BF)
            for ref, new in ((dq, new_dq), (dk, new_dk), (dv, new_dv)):
                ref[rows, window] = jnp.where(mask, new, ref[rows, window])
        return carry

    lax.fori_loop(0, D // HEAD_DIM, head, 0)
    for copy in copies[1:]:
        copy.wait()
    middle = (
        g0[...].astype(F32)
        + nt(dq[...], wq[...])
        + nt(dk[...], wk[...])
        + nt(dv[...], wv[...])
    ).astype(BF)
    out_ref[...] = nn(permutation(64), middle).astype(BF).reshape(8, 64, D)


def temporal(r, wo, wq, wk, wv):
    hbm = pl.BlockSpec(memory_space=pl.ANY)
    vmem = pl.BlockSpec(memory_space=pltpu.VMEM)
    weight = pltpu.VMEM((D, D), BF)
    rows = pltpu.VMEM((512, D), BF)
    return pl.pallas_call(
        temporal_kernel,
        out_shape=jax.ShapeDtypeStruct((8, 64, D), BF),
        in_specs=[vmem, hbm, hbm, hbm, hbm],
        out_specs=vmem,
        scratch_shapes=[weight] * 4 + [rows] * 8 + [pltpu.SemaphoreType.DMA((4,))],
        compiler_params=pltpu.CompilerParams(vmem_limit_bytes=VMEM_LIMIT),
        cost_estimate=pl.CostEstimate(
            flops=20_000_000_000, bytes_accessed=16_000_000, transcendentals=2_000_000
        ),
        name="temporal",
    )(r, wo, wq, wk, wv)


def project_kernel(m_ref, w_ref, middle_ref, gs_ref):
    row = lax.broadcasted_iota(jnp.int32, (512, 512), 0)
    column = lax.broadcasted_iota(jnp.int32, (512, 512), 1)
    frame, block, low = row // 64, (row // 8) % 8, row % 8
    perm = (column == block * 64 + frame * 8 + low).astype(BF)
    middle = nn(perm, m_ref[...].reshape(512, D)).astype(BF)
    middle_ref[...] = middle.reshape(8, 64, D)
    gs = nt(middle, w_ref[...]).astype(BF).reshape(8, 64, D)
    gs_ref[:, 0] = gs[:, :, :HALF]
    gs_ref[:, 1] = gs[:, :, D - HALF :]


def project(m, w):
    vmem = pl.BlockSpec(memory_space=pltpu.VMEM)
    return pl.pallas_call(
        project_kernel,
        out_shape=(
            jax.ShapeDtypeStruct((8, 64, D), BF),
            jax.ShapeDtypeStruct((8, 2, 64, HALF), BF),
        ),
        in_specs=[vmem, vmem],
        out_specs=(vmem, vmem),
        compiler_params=pltpu.CompilerParams(vmem_limit_bytes=VMEM_LIMIT),
        cost_estimate=pl.CostEstimate(
            flops=4_000_000_000, bytes_accessed=8_000_000, transcendentals=0
        ),
        name="project",
    )(m, w)


def spatial_kernel(base_ref, qkv_ref, g_ref, out_ref, qh, kh, vh, gh, dk, dv):
    base = base_ref[0]

    def head(j, carry):
        first = (j // 2) * 128
        window = pl.ds(pl.multiple_of(first, 128), 256)
        mask = lane_mask(1024, base + j * HEAD_DIM - first)
        for dst, src in (
            (qh, qkv_ref[:, 0, :, window]),
            (kh, qkv_ref[:, 1, :, window]),
            (vh, qkv_ref[:, 2, :, window]),
            (gh, g_ref[:, :, window]),
        ):
            src = src.reshape(1024, 256)
            dst[...] = jnp.where(mask, src, jnp.zeros_like(src))
        dk[...] = jnp.zeros_like(dk)
        dv[...] = jnp.zeros_like(dv)

        def block(i, inner):
            rows = pl.ds(pl.multiple_of(i * 256, 256), 256)
            qb, gb = qh[rows], gh[rows]
            s = nt(kh[...], qb) * (SCALE * LOG2E)
            p = jnp.exp2(s - jnp.max(s, axis=0, keepdims=True))
            p = p * (1.0 / jnp.sum(p, axis=0, keepdims=True))
            dp = nt(vh[...], gb)
            delta = jnp.sum(p * dp, axis=0, keepdims=True)
            ds = (p * (dp - delta)).astype(BF)
            dk[...] += nn(ds, qb)
            dv[...] += nn(p.astype(BF), gb)
            new_dq = (tn(ds, kh[...]) * SCALE).astype(BF).reshape(4, 64, 256)
            four = pl.ds(i * 4, 4)
            out_ref[four, 0, :, window] = jnp.where(
                mask[:256].reshape(4, 64, 256), new_dq, out_ref[four, 0, :, window]
            )
            return inner

        lax.fori_loop(0, 4, block, 0)
        deep = mask.reshape(16, 64, 256)
        for a, new in ((1, dk[...] * SCALE), (2, dv[...])):
            out_ref[:, a, :, window] = jnp.where(
                deep, new.astype(BF).reshape(16, 64, 256), out_ref[:, a, :, window]
            )
        return carry

    lax.fori_loop(0, 8, head, 0)


def spatial(base, qkv, g):
    vmem = pl.BlockSpec(memory_space=pltpu.VMEM)
    return pl.pallas_call(
        spatial_kernel,
        out_shape=jax.ShapeDtypeStruct((16, 3, 64, HALF), BF),
        in_specs=[pl.BlockSpec(memory_space=pltpu.SMEM), vmem, vmem],
        out_specs=vmem,
        scratch_shapes=[pltpu.VMEM((1024, 256), BF)] * 4 + [pltpu.VMEM((1024, 256), F32)] * 2,
        compiler_params=pltpu.CompilerParams(vmem_limit_bytes=VMEM_LIMIT),
        cost_estimate=pl.CostEstimate(
            flops=22_000_000_000, bytes_accessed=9_000_000, transcendentals=8_400_000
        ),
        name="spatial",
    )(base, qkv, g)


def unpack_kernel(r_ref, *out_refs):
    lane = lax.broadcasted_iota(jnp.int32, (64, 128), 1)
    for a, out in enumerate(out_refs):
        out[0, :, :512] = r_ref[0, 0, a, :, :512]
        out[0, :, 512:640] = jnp.where(
            lane < 64, r_ref[0, 0, a, :, 512:640], r_ref[0, 1, a, :, :128]
        )
        out[0, :, 640:] = r_ref[0, 1, a, :, 128:]


def unpack(r):
    whole = jax.ShapeDtypeStruct((8, 64, D), BF)
    return pl.pallas_call(
        unpack_kernel,
        out_shape=(whole,) * 3,
        grid=(8,),
        in_specs=[pl.BlockSpec((1, 2, 3, 64, HALF), lambda f: (f, 0, 0, 0, 0))],
        out_specs=(pl.BlockSpec((1, 64, D), lambda f: (f, 0, 0)),) * 3,
        compiler_params=pltpu.CompilerParams(vmem_limit_bytes=VMEM_LIMIT),
        name="unpack",
    )(r)


def exchange(x, axis):
    return lax.all_to_all(x, axis, 0, 0, tiled=True)


def per_device(
    query_time, key_time, value_time, query_space, key_space, value_space, grad_output,
    outproj_time, queryproj_time, keyproj_time, valueproj_time, outproj_space,
):
    t = jnp.stack([query_time, key_time, value_time, grad_output])
    t = t.reshape(4, 8, 8, 8, D).transpose(2, 0, 1, 3, 4).reshape(8, 4, 64, D)
    t = exchange(t, "tm")
    middle = temporal(t, outproj_time, queryproj_time, keyproj_time, valueproj_time)
    middle = exchange(middle, "tm")
    middle_grad, gs = project(middle, outproj_space)
    s = jnp.stack([query_space, key_space, value_space], axis=1)
    s = jnp.stack([s[..., :HALF], s[..., D - HALF :]], axis=1).reshape(16, 3, 64, HALF)
    s = exchange(s, "space")
    gs = exchange(gs.reshape(16, 64, HALF), "space")
    base = (lax.axis_index("space") % 2 * 64).astype(jnp.int32).reshape(1)
    out = exchange(spatial(base, s, gs), "space")
    query_grad, key_grad, value_grad = unpack(out.reshape(8, 2, 3, 64, HALF))
    return query_grad, key_grad, value_grad, middle_grad


def solution(mesh):
    bulk = P("tm", "space", None)
    return jax.shard_map(
        per_device,
        mesh=mesh,
        in_specs=(bulk,) * 7 + (P(),) * 5,
        out_specs=(bulk,) * 4,
        check_vma=False,
    )
```

time: 591 us -> 328 us (0.55)
  the two profiles are of different devices: /device:TPU:111 before, /device:TPU:1 now
where the time goes in v1:
time: 328 us
  blocking collectives  113 us (34%)
  Pallas kernels  102 us (31%)
  waiting for transfers between devices  78.5 us (24%)
  starting transfers between devices  25.7 us (8%)
  local copies, waits for them, and re-layouts  4.14 us (1%)
  other arithmetic  3.62 us (1%)
    all_to_all x2, blocking collectives, exchange(): return lax.all_to_all(x, axis, 0, 0, tiled=True)  113 us
    all_to_all x3, waiting for transfers between devices, exchange(): return lax.all_to_all(x, axis, 0, 0, tiled=True)  78.5 us
    pallas_call x1, Pallas kernels, spatial(): pl.pallas_call(spatial_kernel, out_shape=jax.ShapeDtypeStruct((16, 3, 64,...  55.3 us
    pallas_call x1, Pallas kernels, temporal(): pl.pallas_call(temporal_kernel, out_shape=jax.ShapeDtypeStruct((8, 64, D)...  34.4 us
    all_to_all x3, starting transfers between devices, exchange(): return lax.all_to_all(x, axis, 0, 0, tiled=True)  25.7 us
  transfers between devices with their start and end apart: 3, of which 3 were waited for; matrix products, arithmetic and copies ran while one was open for 1% of the time, Pallas kernels for 2%

profile of v1, /device:TPU:1, one launch (start us, length us, event | category | flops | bytes accessed | tf_op | source)
XLA Modules:
  0.0 327.7 jit_solution(12023227552813224060)
XLA Ops:
  0.6 2.7 copy_bitcast_fusion
  3.3 59.9 %all_to_all.25.r_ref = bf16[8,4,64,1152]{3,2,1,0:T(8,128)(2,1)} all-to-all(bf16[8,4,64,1152]{3,2,1,0:T(8,128)(2,1)S(1)} %copy_bitcast_fusion), channel_id=1, replica_groups=mesh['tm'=8,'space'=16] {'tm'}, dimensions={0} | all-to-all | bytes 9437184 | tf_op jit(solution)/shard_map/all_to_all | solution.py:231
  63.2 0.0 copy-start.3
  63.2 34.4 %temporal.1 = bf16[8,64,1152]{2,1,0:T(8,128)(2,1)} custom-call(bf16[8,4,64,1152]{3,2,1,0:T(8,128)(2,1)} %all_to_all.25.r_ref, bf16[1152,1152]{1,0:T(8,128)(2,1)} %wo_hbm.1, bf16[1152,1152]{1,0:T(8,128)(2,1)} %wq_hbm.1, bf16[1152,1152]{1,0:T(8,128)(2,1)} %wk_hbm.1, bf16[1152,1152]{1,0:T(8,128)(2,1)} %wv_hbm.1), custom_call_target="tpu_custom_call" | custom-call | flops 20000000000 | bytes 16000000 | tf_op jit(solution)/shard_map/temporal/pallas_call | solution.py:100
  97.6 0.0 copy-start.1
  97.6 0.0 copy-start.2
  97.6 4.4 %all-to-all-start.2 = ((bf16[8,64,1152]{2,1,0:T(8,128)(2,1)}), bf16[8,64,1152]{2,1,0:T(8,128)(2,1)}, u32[]{:S(2)}, u32[]{:S(2)}) async-start(bf16[8,64,1152]{2,1,0:T(8,128)(2,1)} %temporal.1), calls=%async_computation.2 | async-start | bytes 2359296 | tf_op jit(solution)/shard_map/all_to_all | solution.py:231
  102.0 0.0 copy-done.3
  102.0 0.0 copy-done.1
  102.0 0.0 copy-done.2
  102.0 0.5 pad_maximum_fusion.2
  102.6 0.7 slice_bitcast_fusion.1
  103.3 0.4 pad_maximum_fusion.1
  103.7 2.3 copy.16
  106.0 13.3 %all-to-all-done.2.m_ref = bf16[8,64,1152]{2,1,0:T(8,128)(2,1)} async-done(((bf16[8,64,1152]{2,1,0:T(8,128)(2,1)}), bf16[8,64,1152]{2,1,0:T(8,128)(2,1)}, u32[]{:S(2)}, u32[]{:S(2)}) %all-to-all-start.2) | async-done | bytes 1179680 | tf_op jit(solution)/shard_map/all_to_all | solution.py:231
  119.2 8.5 %all-to-all-start = ((bf16[16,3,64,640]{3,2,1,0:T(8,128)(2,1)}), bf16[16,3,64,640]{3,2,1,0:T(8,128)(2,1)}, u32[]{:S(2)}, u32[]{:S(2)}) async-start(bf16[16,3,64,640]{3,2,1,0:T(8,128)(2,1)} %bitcast.19), calls=%async_computation | async-start | bytes 7864320 | tf_op jit(solution)/shard_map/all_to_all | solution.py:231
  127.8 5.8 %project.1 = (bf16[8,64,1152]{2,1,0:T(8,128)(2,1)}, bf16[8,2,64,640]{3,2,1,0:T(8,128)(2,1)}) custom-call(bf16[8,64,1152]{2,1,0:T(8,128)(2,1)} %all-to-all-done.2.m_ref, bf16[1152,1152]{1,0:T(8,128)(2,1)} %w_ref.1), custom_call_target="tpu_custom_call" | custom-call | flops 4000000000 | bytes 8000000 | tf_op jit(solution)/shard_map/project/pallas_call | solution.py:128
  133.6 45.1 %all-to-all-done.qkv_ref = bf16[16,3,64,640]{3,2,1,0:T(8,128)(2,1)} async-done(((bf16[16,3,64,640]{3,2,1,0:T(8,128)(2,1)}), bf16[16,3,64,640]{3,2,1,0:T(8,128)(2,1)}, u32[]{:S(2)}, u32[]{:S(2)}) %all-to-all-start) | async-done | bytes 3932192 | tf_op jit(solution)/shard_map/all_to_all | solution.py:231
  178.7 12.8 %all-to-all-start.3 = ((bf16[16,64,640]{2,1,0:T(8,128)(2,1)}), bf16[16,64,640]{2,1,0:T(8,128)(2,1)S(1)}, u32[]{:S(2)}, u32[]{:S(2)}) async-start(bf16[16,64,640]{2,1,0:T(8,128)(2,1)} %bitcast.21), calls=%async_computation.3 | async-start | bytes 2621440 | tf_op jit(solution)/shard_map/all_to_all | solution.py:231
  191.5 20.0 %all-to-all-done.3.g_ref = bf16[16,64,640]{2,1,0:T(8,128)(2,1)S(1)} async-done(((bf16[16,64,640]{2,1,0:T(8,128)(2,1)}), bf16[16,64,640]{2,1,0:T(8,128)(2,1)S(1)}, u32[]{:S(2)}, u32[]{:S(2)}) %all-to-all-start.3) | async-done | bytes 1310752 | tf_op jit(solution)/shard_map/all_to_all | solution.py:231
  211.6 0.0 copy-start
  211.6 1.1 copy-done
  212.7 55.3 %spatial.1 = bf16[16,3,64,640]{3,2,1,0:T(8,128)(2,1)} custom-call(s32[1]{0:T(128)} %bitcast.base_ref, bf16[16,3,64,640]{3,2,1,0:T(8,128)(2,1)} %all-to-all-done.qkv_ref, bf16[16,64,640]{2,1,0:T(8,128)(2,1)} %copy-done), custom_call_target="tpu_custom_call" | custom-call | flops 22000001024 | bytes 9000000 | tf_op jit(solution)/shard_map/spatial/pallas_call | solution.py:193
  268.0 53.3 %all_to_all.26 = bf16[16,3,64,640]{3,2,1,0:T(8,128)(2,1)} all-to-all(bf16[16,3,64,640]{3,2,1,0:T(8,128)(2,1)} %spatial.1), channel_id=1, replica_groups=mesh['tm'=8,'space'=16] {'space'}, dimensions={0} | all-to-all | bytes 7864320 | tf_op jit(solution)/shard_map/all_to_all | solution.py:231
  321.3 6.4 %unpack.1 = (bf16[8,64,1152]{2,1,0:T(8,128)(2,1)}, bf16[8,64,1152]{2,1,0:T(8,128)(2,1)}, bf16[8,64,1152]{2,1,0:T(8,128)(2,1)}) custom-call(bf16[8,2,3,64,640]{4,3,2,1,0:T(8,128)(2,1)} %bitcast.20), custom_call_target="tpu_custom_call" | custom-call | tf_op jit(solution)/shard_map/unpack/pallas_call | solution.py:219
Async XLA Ops:
  63.2 38.8 %copy-start.3 = (bf16[8,64,1152]{2,1,0:T(8,128)(2,1)S(1)}, bf16[8,64,1152]{2,1,0:T(8,128)(2,1)}, u32[]{:S(2)}) copy-start(bf16[8,64,1152]{2,1,0:T(8,128)(2,1)} %param.15) | copy-start | bytes 3538948
  97.6 4.4 %copy-start.1 = (bf16[8,64,1152]{2,1,0:T(8,128)(2,1)S(1)}, bf16[8,64,1152]{2,1,0:T(8,128)(2,1)}, u32[]{:S(2)}) copy-start(bf16[8,64,1152]{2,1,0:T(8,128)(2,1)} %param.17) | copy-start | bytes 3538948
  97.6 4.4 %copy-start.2 = (bf16[8,64,1152]{2,1,0:T(8,128)(2,1)S(1)}, bf16[8,64,1152]{2,1,0:T(8,128)(2,1)}, u32[]{:S(2)}) copy-start(bf16[8,64,1152]{2,1,0:T(8,128)(2,1)} %param.16) | copy-start | bytes 3538948
  97.6 21.6 %all-to-all-start.2 = ((bf16[8,64,1152]{2,1,0:T(8,128)(2,1)}), bf16[8,64,1152]{2,1,0:T(8,128)(2,1)}, u32[]{:S(2)}, u32[]{:S(2)}) async-start(bf16[8,64,1152]{2,1,0:T(8,128)(2,1)} %temporal.1), calls=%async_computation.2 | async-start | bytes 2359296 | tf_op jit(solution)/shard_map/all_to_all | solution.py:231
  119.2 59.5 %all-to-all-start = ((bf16[16,3,64,640]{3,2,1,0:T(8,128)(2,1)}), bf16[16,3,64,640]{3,2,1,0:T(8,128)(2,1)}, u32[]{:S(2)}, u32[]{:S(2)}) async-start(bf16[16,3,64,640]{3,2,1,0:T(8,128)(2,1)} %bitcast.19), calls=%async_computation | async-start | bytes 7864320 | tf_op jit(solution)/shard_map/all_to_all | solution.py:231
  178.7 32.9 %all-to-all-start.3 = ((bf16[16,64,640]{2,1,0:T(8,128)(2,1)}), bf16[16,64,640]{2,1,0:T(8,128)(2,1)S(1)}, u32[]{:S(2)}, u32[]{:S(2)}) async-start(bf16[16,64,640]{2,1,0:T(8,128)(2,1)} %bitcast.21), calls=%async_computation.3 | async-start | bytes 2621440 | tf_op jit(solution)/shard_map/all_to_all | solution.py:231
  211.6 1.1 copy-start

commit v2 on v1

--- a/solution.py
+++ b/solution.py
@@ -111,7 +111,7 @@
     )(r, wo, wq, wk, wv)
 
 
-def project_kernel(m_ref, w_ref, middle_ref, gs_ref):
+def project_kernel(m_ref, w_ref, v_ref, middle_ref, vg_ref):
     row = lax.broadcasted_iota(jnp.int32, (512, 512), 0)
     column = lax.broadcasted_iota(jnp.int32, (512, 512), 1)
     frame, block, low = row // 64, (row // 8) % 8, row % 8
@@ -119,110 +119,132 @@
     middle = nn(perm, m_ref[...].reshape(512, D)).astype(BF)
     middle_ref[...] = middle.reshape(8, 64, D)
     gs = nt(middle, w_ref[...]).astype(BF).reshape(8, 64, D)
-    gs_ref[:, 0] = gs[:, :, :HALF]
-    gs_ref[:, 1] = gs[:, :, D - HALF :]
-
-
-def project(m, w):
+    for half, lanes in enumerate((slice(0, HALF), slice(D - HALF, D))):
+        vg_ref[:, half, 0] = v_ref[:, :, lanes]
+        vg_ref[:, half, 1] = gs[:, :, lanes]
+
+
+def project(m, w, v):
     vmem = pl.BlockSpec(memory_space=pltpu.VMEM)
     return pl.pallas_call(
         project_kernel,
         out_shape=(
             jax.ShapeDtypeStruct((8, 64, D), BF),
-            jax.ShapeDtypeStruct((8, 2, 64, HALF), BF),
-        ),
-        in_specs=[vmem, vmem],
+            jax.ShapeDtypeStruct((8, 2, 2, 64, HALF), BF),
+        ),
+        in_specs=[vmem, vmem, vmem],
         out_specs=(vmem, vmem),
         compiler_params=pltpu.CompilerParams(vmem_limit_bytes=VMEM_LIMIT),
         cost_estimate=pl.CostEstimate(
             flops=4_000_000_000, bytes_accessed=8_000_000, transcendentals=0
         ),
         name="project",
-    )(m, w)
-
-
-def spatial_kernel(base_ref, qkv_ref, g_ref, out_ref, qh, kh, vh, gh, dk, dv):
-    base = base_ref[0]
-
-    def head(j, carry):
-        first = (j // 2) * 128
-        window = pl.ds(pl.multiple_of(first, 128), 256)
-        mask = lane_mask(1024, base + j * HEAD_DIM - first)
-        for dst, src in (
-            (qh, qkv_ref[:, 0, :, window]),
-            (kh, qkv_ref[:, 1, :, window]),
-            (vh, qkv_ref[:, 2, :, window]),
-            (gh, g_ref[:, :, window]),
-        ):
-            src = src.reshape(1024, 256)
-            dst[...] = jnp.where(mask, src, jnp.zeros_like(src))
-        dk[...] = jnp.zeros_like(dk)
-        dv[...] = jnp.zeros_like(dv)
-
-        def block(i, inner):
-            rows = pl.ds(pl.multiple_of(i * 256, 256), 256)
-            qb, gb = qh[rows], gh[rows]
-            s = nt(kh[...], qb) * (SCALE * LOG2E)
-            p = jnp.exp2(s - jnp.max(s, axis=0, keepdims=True))
-            p = p * (1.0 / jnp.sum(p, axis=0, keepdims=True))
-            dp = nt(vh[...], gb)
-            delta = jnp.sum(p * dp, axis=0, keepdims=True)
-            ds = (p * (dp - delta)).astype(BF)
-            dk[...] += nn(ds, qb)
-            dv[...] += nn(p.astype(BF), gb)
-            new_dq = (tn(ds, kh[...]) * SCALE).astype(BF).reshape(4, 64, 256)
-            four = pl.ds(i * 4, 4)
-            out_ref[four, 0, :, window] = jnp.where(
-                mask[:256].reshape(4, 64, 256), new_dq, out_ref[four, 0, :, window]
-            )
-            return inner
-
-        lax.fori_loop(0, 4, block, 0)
-        deep = mask.reshape(16, 64, 256)
-        for a, new in ((1, dk[...] * SCALE), (2, dv[...])):
-            out_ref[:, a, :, window] = jnp.where(
-                deep, new.astype(BF).reshape(16, 64, 256), out_ref[:, a, :, window]
-            )
-        return carry
-
-    lax.fori_loop(0, 8, head, 0)
-
-
-def spatial(base, qkv, g):
-    vmem = pl.BlockSpec(memory_space=pltpu.VMEM)
-    return pl.pallas_call(
-        spatial_kernel,
+    )(m, w, v)
+
+
+def head_window(j, base):
+    first = (j // 2) * 128
+    return pl.ds(pl.multiple_of(first, 128), 256), base + j * HEAD_DIM - first
+
+
+def masked(ref, a, window, mask):
+    x = ref[:, a, :, window].reshape(1024, 256)
+    return jnp.where(mask, x, jnp.zeros_like(x))
+
+
+def probs_kernel(base_ref, qk_ref, p_ref, kh):
+    window, low = head_window(pl.program_id(0), base_ref[0])
+    kh[...] = masked(qk_ref, 1, window, lane_mask(1024, low))
+    for i in range(4):
+        rows = slice(i * 256, (i + 1) * 256)
+        qb = qk_ref[4 * i : 4 * i + 4, 0, :, window].reshape(256, 256)
+        s = nt(kh[...], qb) * (SCALE * LOG2E)
+        p = jnp.exp2(s - jnp.max(s, axis=0, keepdims=True))
+        p_ref[0, :, rows] = (p * (1.0 / jnp.sum(p, axis=0, keepdims=True))).astype(BF)
+
+
+def probs(base, qk):
+    return pl.pallas_call(
+        probs_kernel,
+        out_shape=jax.ShapeDtypeStruct((8, 1024, 1024), BF),
+        grid=(8,),
+        in_specs=[
+            pl.BlockSpec(memory_space=pltpu.SMEM),
+            pl.BlockSpec((16, 2, 64, HALF), lambda j: (0, 0, 0, 0)),
+        ],
+        out_specs=pl.BlockSpec((1, 1024, 1024), lambda j: (j, 0, 0)),
+        scratch_shapes=[pltpu.VMEM((1024, 256), BF)],
+        compiler_params=pltpu.CompilerParams(vmem_limit_bytes=VMEM_LIMIT),
+        cost_estimate=pl.CostEstimate(
+            flops=20_000_000_000, bytes_accessed=20_000_000, transcendentals=8_400_000
+        ),
+        name="probs",
+    )(base, qk)
+
+
+def grads_kernel(base_ref, qk_ref, vg_ref, p_ref, out_ref, qh, kh, vh, gh, ds):
+    window, low = head_window(pl.program_id(0), base_ref[0])
+    mask = lane_mask(1024, low)
+    for dst, ref, a in ((qh, qk_ref, 0), (kh, qk_ref, 1), (vh, vg_ref, 0), (gh, vg_ref, 1)):
+        dst[...] = masked(ref, a, window, mask)
+    deep = mask.reshape(16, 64, 256)
+
+    def put(a, new):
+        new = new.astype(BF).reshape(16, 64, 256)
+        out_ref[:, a, :, window] = jnp.where(deep, new, out_ref[:, a, :, window])
+
+    for i in range(4):
+        rows = slice(i * 256, (i + 1) * 256)
+        dp = nt(vh[...], gh[rows])
+        p = p_ref[0, :, rows].astype(F32)
+        delta = jnp.sum(p * dp, axis=0, keepdims=True)
+        ds[:, rows] = (p * (dp - delta)).astype(BF)
+    put(2, nn(p_ref[0], gh[...]))
+    put(1, nn(ds[...], qh[...]) * SCALE)
+    put(0, tn(ds[...], kh[...]) * SCALE)
+
+
+def grads(base, qk, vg, p):
+    whole = pl.BlockSpec((16, 2, 64, HALF), lambda j: (0, 0, 0, 0))
+    return pl.pallas_call(
+        grads_kernel,
         out_shape=jax.ShapeDtypeStruct((16, 3, 64, HALF), BF),
-        in_specs=[pl.BlockSpec(memory_space=pltpu.SMEM), vmem, vmem],
-        out_specs=vmem,
-        scratch_shapes=[pltpu.VMEM((1024, 256), BF)] * 4 + [pltpu.VMEM((1024, 256), F32)] * 2,
-        compiler_params=pltpu.CompilerParams(vmem_limit_bytes=VMEM_LIMIT),
-        cost_estimate=pl.CostEstimate(
-            flops=22_000_000_000, bytes_accessed=9_000_000, transcendentals=8_400_000
-        ),
-        name="spatial",
-    )(base, qkv, g)
+        grid=(8,),
+        in_specs=[
+            pl.BlockSpec(memory_space=pltpu.SMEM),
+            whole,
+            whole,
+            pl.BlockSpec((1, 1024, 1024), lambda j: (j, 0, 0)),
+        ],
+        out_specs=pl.BlockSpec((16, 3, 64, HALF), lambda j: (0, 0, 0, 0)),
+        scratch_shapes=[pltpu.VMEM((1024, 256), BF)] * 4 + [pltpu.VMEM((1024, 1024), BF)],
+        compiler_params=pltpu.CompilerParams(vmem_limit_bytes=VMEM_LIMIT),
+        cost_estimate=pl.CostEstimate(
+            flops=22_000_000_000, bytes_accessed=26_000_000, transcendentals=0
+        ),
+        name="grads",
+    )(base, qk, vg, p)
 
 
 def unpack_kernel(r_ref, *out_refs):
-    lane = lax.broadcasted_iota(jnp.int32, (64, 128), 1)
+    lane = lax.broadcasted_iota(jnp.int32, (8, 64, 128), 2)
     for a, out in enumerate(out_refs):
-        out[0, :, :512] = r_ref[0, 0, a, :, :512]
-        out[0, :, 512:640] = jnp.where(
-            lane < 64, r_ref[0, 0, a, :, 512:640], r_ref[0, 1, a, :, :128]
+        out[:, :, :512] = r_ref[:, 0, a, :, :512]
+        out[:, :, 512:640] = jnp.where(
+            lane < 64, r_ref[:, 0, a, :, 512:640], r_ref[:, 1, a, :, :128]
         )
-        out[0, :, 640:] = r_ref[0, 1, a, :, 128:]
+        out[:, :, 640:] = r_ref[:, 1, a, :, 128:]
 
 
 def unpack(r):
     whole = jax.ShapeDtypeStruct((8, 64, D), BF)
+    vmem = pl.BlockSpec(memory_space=pltpu.VMEM)
     return pl.pallas_call(
         unpack_kernel,
         out_shape=(whole,) * 3,
-        grid=(8,),
-        in_specs=[pl.BlockSpec((1, 2, 3, 64, HALF), lambda f: (f, 0, 0, 0, 0))],
-        out_specs=(pl.BlockSpec((1, 64, D), lambda f: (f, 0, 0)),) * 3,
-        compiler_params=pltpu.CompilerParams(vmem_limit_bytes=VMEM_LIMIT),
+        in_specs=[vmem],
+        out_specs=(vmem,) * 3,
+        compiler_params=pltpu.CompilerParams(vmem_limit_bytes=32 * 1024 * 1024),
         name="unpack",
     )(r)
 
@@ -235,18 +257,22 @@
     query_time, key_time, value_time, query_space, key_space, value_space, grad_output,
     outproj_time, queryproj_time, keyproj_time, valueproj_time, outproj_space,
 ):
+    base = (lax.axis_index("space") % 2 * 64).astype(jnp.int32).reshape(1)
     t = jnp.stack([query_time, key_time, value_time, grad_output])
     t = t.reshape(4, 8, 8, 8, D).transpose(2, 0, 1, 3, 4).reshape(8, 4, 64, D)
     t = exchange(t, "tm")
+    qk = jnp.stack([query_space, key_space], axis=1)
+    qk = jnp.stack([qk[..., :HALF], qk[..., D - HALF :]], axis=1).reshape(16, 2, 64, HALF)
+    qk, t = lax.optimization_barrier((qk, t))
+    qk = exchange(qk, "space")
     middle = temporal(t, outproj_time, queryproj_time, keyproj_time, valueproj_time)
+    middle, qk = lax.optimization_barrier((middle, qk))
     middle = exchange(middle, "tm")
-    middle_grad, gs = project(middle, outproj_space)
-    s = jnp.stack([query_space, key_space, value_space], axis=1)
-    s = jnp.stack([s[..., :HALF], s[..., D - HALF :]], axis=1).reshape(16, 3, 64, HALF)
-    s = exchange(s, "space")
-    gs = exchange(gs.reshape(16, 64, HALF), "space")
-    base = (lax.axis_index("space") % 2 * 64).astype(jnp.int32).reshape(1)
-    out = exchange(spatial(base, s, gs), "space")
+    middle_grad, vg = project(middle, outproj_space, value_space)
+    vg, qk = lax.optimization_barrier((vg, qk))
+    p = probs(base, qk)
+    vg = exchange(vg.reshape(16, 2, 64, HALF), "space")
+    out = exchange(grads(base, qk, vg, p), "space")
     query_grad, key_grad, value_grad = unpack(out.reshape(8, 2, 3, 64, HALF))
     return query_grad, key_grad, value_grad, middle_grad
 

time: 328 us -> 285 us (0.87)
  blocking collectives: 113 us -> 91.5 us
  Pallas kernels: 102 us -> 88.5 us
  waiting for transfers between devices: 78.5 us -> 69.3 us
    all_to_all x2, blocking collectives: 113 us -> 91.5 us  [exchange(): return lax.all_to_all(x, axis, 0, 0, tiled=True)]
    pallas_call x2 -> x3, Pallas kernels: 61.7 us -> 47.7 us  [the longest x1 27 us: grads(): pl.pallas_call(grads_kernel, out_shape=jax.ShapeDtypeStruct((16, 3, 64, H...]
    all_to_all x3, waiting for transfers between devices: 78.5 us -> 69.3 us  [exchange(): return lax.all_to_all(x, axis, 0, 0, tiled=True)]
  transfers between devices with their start and end apart: 3 -> 3, of which waited for: 3 -> 3; matrix products, arithmetic and copies ran while one was open for 1% -> 1% of each run, Pallas kernels for 2% -> 19%
where the time goes in v2:
time: 285 us
  blocking collectives  91.5 us (32%)
  Pallas kernels  88.5 us (31%)
  waiting for transfers between devices  69.3 us (24%)
  starting transfers between devices  25.1 us (9%)
  other arithmetic  6.34 us (2%)
  local copies, waits for them, and re-layouts  3.27 us (1%)
    all_to_all x2, blocking collectives, exchange(): return lax.all_to_all(x, axis, 0, 0, tiled=True)  91.5 us
    all_to_all x3, waiting for transfers between devices, exchange(): return lax.all_to_all(x, axis, 0, 0, tiled=True)  69.3 us
    pallas_call x1, Pallas kernels, temporal(): pl.pallas_call(temporal_kernel, out_shape=jax.ShapeDtypeStruct((8, 64, D)...  34.3 us
    pallas_call x1, Pallas kernels, grads(): pl.pallas_call(grads_kernel, out_shape=jax.ShapeDtypeStruct((16, 3, 64, H...  27 us
    all_to_all x3, starting transfers between devices, exchange(): return lax.all_to_all(x, axis, 0, 0, tiled=True)  25.1 us
    pallas_call x1, Pallas kernels, probs(): pl.pallas_call(probs_kernel, out_shape=jax.ShapeDtypeStruct((8, 1024, 102...  18.6 us
    pallas_call x1, Pallas kernels, project(): pl.pallas_call(project_kernel, out_shape=(jax.ShapeDtypeStruct((8, 64, D)...  6.53 us
  transfers between devices with their start and end apart: 3, of which 3 were waited for; matrix products, arithmetic and copies ran while one was open for 1% of the time, Pallas kernels for 19%

profile of v2, /device:TPU:1, one launch (start us, length us, event | category | flops | bytes accessed | tf_op | source)
XLA Modules:
  0.0 284.7 jit_solution(9407891366255443598)
XLA Ops:
  0.6 5.7 %copy_bitcast_fusion = bf16[8,4,64,1152]{3,2,1,0:T(8,128)(2,1)} fusion(bf16[1,8,8,8,1152]{4,3,2,1,0:T(8,128)(2,1)} %bitcast.20, bf16[1,8,8,8,1152]{4,3,2,1,0:T(8,128)(2,1)} %bitcast.21, bf16[1,8,8,8,1152]{4,3,2,1,0:T(8,128)(2,1)} %bitcast.22, bf16[1,8,8,8,1152]{4,3,2,1,0:T(8,128)(2,1)} %bitcast.23), kind=kLoop, calls=%fused_computation.1 | loop fusion | flops 7077888 | bytes 9437184 | tf_op jit(solution)/shard_map/reshape | solution.py:262
  6.3 0.0 copy-start.2
  6.3 0.0 copy-start.3
  6.3 6.0 %all-to-all-start = ((bf16[8,4,64,1152]{3,2,1,0:T(8,128)(2,1)}), bf16[8,4,64,1152]{3,2,1,0:T(8,128)(2,1)}, u32[]{:S(2)}, u32[]{:S(2)}) async-start(bf16[8,4,64,1152]{3,2,1,0:T(8,128)(2,1)} %copy_bitcast_fusion), calls=%async_computation | async-start | bytes 9437184 | tf_op jit(solution)/shard_map/all_to_all | solution.py:253
  12.3 0.0 copy-done.2
  12.3 0.0 copy-done.3
  12.3 0.4 fusion.1
  12.7 0.3 pad_maximum_fusion.1
  13.0 1.7 copy.16
  14.7 52.8 %all-to-all-done.r_ref = bf16[8,4,64,1152]{3,2,1,0:T(8,128)(2,1)} async-done(((bf16[8,4,64,1152]{3,2,1,0:T(8,128)(2,1)}), bf16[8,4,64,1152]{3,2,1,0:T(8,128)(2,1)}, u32[]{:S(2)}, u32[]{:S(2)}) %all-to-all-start) | async-done | bytes 4718624 | tf_op jit(solution)/shard_map/all_to_all | solution.py:253
  67.6 8.5 %all-to-all-start.1 = ((bf16[16,2,64,640]{3,2,1,0:T(8,128)(2,1)}), bf16[16,2,64,640]{3,2,1,0:T(8,128)(2,1)S(1)}, u32[]{:S(2)}, u32[]{:S(2)}) async-start(bf16[16,2,64,640]{3,2,1,0:T(8,128)(2,1)} %bitcast.5), calls=%async_computation.1 | async-start | bytes 5242880 | tf_op jit(solution)/shard_map/all_to_all | solution.py:253
  76.1 34.3 %temporal.1 = bf16[8,64,1152]{2,1,0:T(8,128)(2,1)} custom-call(bf16[8,4,64,1152]{3,2,1,0:T(8,128)(2,1)} %all-to-all-done.r_ref, bf16[1152,1152]{1,0:T(8,128)(2,1)} %wo_hbm.1, bf16[1152,1152]{1,0:T(8,128)(2,1)} %wq_hbm.1, bf16[1152,1152]{1,0:T(8,128)(2,1)} %wk_hbm.1, bf16[1152,1152]{1,0:T(8,128)(2,1)} %wv_hbm.1), custom_call_target="tpu_custom_call" | custom-call | flops 20000000000 | bytes 16000000 | tf_op jit(solution)/shard_map/temporal/pallas_call | solution.py:100
  110.4 0.4 all-to-all-done.1.qk_ref
  110.8 0.0 copy-start
  110.8 34.5 %all_to_all.25.m_ref = bf16[8,64,1152]{2,1,0:T(8,128)(2,1)} all-to-all(bf16[8,64,1152]{2,1,0:T(8,128)(2,1)} %temporal.1), channel_id=1, replica_groups=mesh['tm'=8,'space'=16] {'tm'}, dimensions={0} | all-to-all | bytes 2359296 | tf_op jit(solution)/shard_map/all_to_all | solution.py:253
  145.3 6.5 %project.1 = (bf16[8,64,1152]{2,1,0:T(8,128)(2,1)}, bf16[8,2,2,64,640]{4,3,2,1,0:T(8,128)(2,1)}) custom-call(bf16[8,64,1152]{2,1,0:T(8,128)(2,1)} %all_to_all.25.m_ref, bf16[1152,1152]{1,0:T(8,128)(2,1)} %w_ref.1, bf16[8,64,1152]{2,1,0:T(8,128)(2,1)} %v_ref.1), custom_call_target="tpu_custom_call" | custom-call | flops 4000000000 | bytes 8000000 | tf_op jit(solution)/shard_map/project/pallas_call | solution.py:129
  151.8 0.0 copy-done
  151.8 10.5 %all-to-all-start.3 = ((bf16[16,2,64,640]{3,2,1,0:T(8,128)(2,1)}), bf16[16,2,64,640]{3,2,1,0:T(8,128)(2,1)S(1)}, u32[]{:S(2)}, u32[]{:S(2)}) async-start(bf16[16,2,64,640]{3,2,1,0:T(8,128)(2,1)} %bitcast.19), calls=%async_computation.3 | async-start | bytes 5242880 | tf_op jit(solution)/shard_map/all_to_all | solution.py:253
  162.4 18.6 %probs.1.p_ref = bf16[8,1024,1024]{2,1,0:T(8,128)(2,1)} custom-call(s32[1]{0:T(128)} %bitcast.base_ref, bf16[16,2,64,640]{3,2,1,0:T(8,128)(2,1)} %copy-done), custom_call_target="tpu_custom_call" | custom-call | flops 20000000000 | bytes 20000000 | tf_op jit(solution)/shard_map/probs/pallas_call | solution.py:167
  181.0 16.1 %all-to-all-done.3.vg_ref = bf16[16,2,64,640]{3,2,1,0:T(8,128)(2,1)S(1)} async-done(((bf16[16,2,64,640]{3,2,1,0:T(8,128)(2,1)}), bf16[16,2,64,640]{3,2,1,0:T(8,128)(2,1)S(1)}, u32[]{:S(2)}, u32[]{:S(2)}) %all-to-all-start.3) | async-done | bytes 2621472 | tf_op jit(solution)/shard_map/all_to_all | solution.py:253
  197.1 0.0 copy-start.1
  197.1 1.5 copy-done.1
  198.6 27.0 %grads.1 = bf16[16,3,64,640]{3,2,1,0:T(8,128)(2,1)} custom-call(s32[1]{0:T(128)} %bitcast.base_ref, bf16[16,2,64,640]{3,2,1,0:T(8,128)(2,1)} %copy-done, bf16[16,2,64,640]{3,2,1,0:T(8,128)(2,1)} %copy-done.1, bf16[8,1024,1024]{2,1,0:T(8,128)(2,1)} %probs.1.p_ref), custom_call_target="tpu_custom_call" | custom-call | flops 22000001024 | bytes 26000000 | tf_op jit(solution)/shard_map/grads/pallas_call | solution.py:209
  225.6 57.0 %all_to_all.26 = bf16[16,3,64,640]{3,2,1,0:T(8,128)(2,1)S(1)} all-to-all(bf16[16,3,64,640]{3,2,1,0:T(8,128)(2,1)} %grads.1), channel_id=1, replica_groups=mesh['tm'=8,'space'=16] {'space'}, dimensions={0} | all-to-all | bytes 7864320 | tf_op jit(solution)/shard_map/all_to_all | solution.py:253
  282.6 2.1 unpack.1
Async XLA Ops:
  6.3 6.0 %copy-start.2 = (bf16[8,64,1152]{2,1,0:T(8,128)(2,1)S(1)}, bf16[8,64,1152]{2,1,0:T(8,128)(2,1)}, u32[]{:S(2)}) copy-start(bf16[8,64,1152]{2,1,0:T(8,128)(2,1)} %param.15) | copy-start | bytes 3538948
  6.3 6.0 %copy-start.3 = (bf16[8,64,1152]{2,1,0:T(8,128)(2,1)S(1)}, bf16[8,64,1152]{2,1,0:T(8,128)(2,1)}, u32[]{:S(2)}) copy-start(bf16[8,64,1152]{2,1,0:T(8,128)(2,1)} %param.16) | copy-start | bytes 3538948
  6.3 61.2 %all-to-all-start = ((bf16[8,4,64,1152]{3,2,1,0:T(8,128)(2,1)}), bf16[8,4,64,1152]{3,2,1,0:T(8,128)(2,1)}, u32[]{:S(2)}, u32[]{:S(2)}) async-start(bf16[8,4,64,1152]{3,2,1,0:T(8,128)(2,1)} %copy_bitcast_fusion), calls=%async_computation | async-start | bytes 9437184 | tf_op jit(solution)/shard_map/all_to_all | solution.py:253
  67.6 43.2 %all-to-all-start.1 = ((bf16[16,2,64,640]{3,2,1,0:T(8,128)(2,1)}), bf16[16,2,64,640]{3,2,1,0:T(8,128)(2,1)S(1)}, u32[]{:S(2)}, u32[]{:S(2)}) async-start(bf16[16,2,64,640]{3,2,1,0:T(8,128)(2,1)} %bitcast.5), calls=%async_computation.1 | async-start | bytes 5242880 | tf_op jit(solution)/shard_map/all_to_all | solution.py:253
  110.8 41.0 %copy-start = (bf16[16,2,64,640]{3,2,1,0:T(8,128)(2,1)}, bf16[16,2,64,640]{3,2,1,0:T(8,128)(2,1)S(1)}, u32[]{:S(2)}) copy-start(bf16[16,2,64,640]{3,2,1,0:T(8,128)(2,1)S(1)} %all-to-all-done.1.qk_ref) | copy-start | bytes 7864324
  151.8 45.2 %all-to-all-start.3 = ((bf16[16,2,64,640]{3,2,1,0:T(8,128)(2,1)}), bf16[16,2,64,640]{3,2,1,0:T(8,128)(2,1)S(1)}, u32[]{:S(2)}, u32[]{:S(2)}) async-start(bf16[16,2,64,640]{3,2,1,0:T(8,128)(2,1)} %bitcast.19), calls=%async_computation.3 | async-start | bytes 5242880 | tf_op jit(solution)/shard_map/all_to_all | solution.py:253
  197.1 1.5 copy-start.1

commit v3 on v2

--- a/solution.py
+++ b/solution.py
@@ -7,7 +7,7 @@
 
 HEAD_DIM = 72
 D = 1152
-HALF = 640
+ROWS = 288
 SCALE = HEAD_DIM**-0.5
 LOG2E = 1.4426950408889634
 BF = jnp.bfloat16
@@ -111,6 +111,46 @@
     )(r, wo, wq, wk, wv)
 
 
+def native(rows, half):
+    return lax.broadcasted_iota(jnp.int32, (rows, 128), 1) // 64 == half
+
+
+def rolled(x):
+    return pltpu.roll(x.astype(F32), 64, 1).astype(BF)
+
+
+def pack_rows(x, half, put):
+    for b in range(4):
+        tile = b + 5 * half
+        put(b * 64, x[:, tile * 128 : tile * 128 + 128])
+    shared = x[:, 512:640]
+    put(256, jnp.where(native(32, half), shared[:32], rolled(shared[32:])))
+
+
+def pack_kernel(*refs):
+    *in_refs, out_ref = refs
+    for f in range(8):
+        for a, ref in enumerate(in_refs):
+            for half in range(2):
+
+                def put(row, value):
+                    out_ref[f, half, a, row : row + value.shape[0]] = value
+
+                pack_rows(ref[f], half, put)
+
+
+def pack(*arrays):
+    vmem = pl.BlockSpec(memory_space=pltpu.VMEM)
+    return pl.pallas_call(
+        pack_kernel,
+        out_shape=jax.ShapeDtypeStruct((8, 2, len(arrays), ROWS, 128), BF),
+        in_specs=[vmem] * len(arrays),
+        out_specs=vmem,
+        compiler_params=pltpu.CompilerParams(vmem_limit_bytes=32 * 1024 * 1024),
+        name="pack",
+    )(*arrays)
+
+
 def project_kernel(m_ref, w_ref, v_ref, middle_ref, vg_ref):
     row = lax.broadcasted_iota(jnp.int32, (512, 512), 0)
     column = lax.broadcasted_iota(jnp.int32, (512, 512), 1)
@@ -118,10 +158,15 @@
     perm = (column == block * 64 + frame * 8 + low).astype(BF)
     middle = nn(perm, m_ref[...].reshape(512, D)).astype(BF)
     middle_ref[...] = middle.reshape(8, 64, D)
-    gs = nt(middle, w_ref[...]).astype(BF).reshape(8, 64, D)
-    for half, lanes in enumerate((slice(0, HALF), slice(D - HALF, D))):
-        vg_ref[:, half, 0] = v_ref[:, :, lanes]
-        vg_ref[:, half, 1] = gs[:, :, lanes]
+    gs = nt(middle, w_ref[...]).astype(BF)
+    for f in range(8):
+        for a, x in enumerate((v_ref[f], gs[f * 64 : f * 64 + 64])):
+            for half in range(2):
+
+                def put(row, value):
+                    vg_ref[f, half, a, row : row + value.shape[0]] = value
+
+                pack_rows(x, half, put)
 
 
 def project(m, w, v):
@@ -130,7 +175,7 @@
         project_kernel,
         out_shape=(
             jax.ShapeDtypeStruct((8, 64, D), BF),
-            jax.ShapeDtypeStruct((8, 2, 2, 64, HALF), BF),
+            jax.ShapeDtypeStruct((8, 2, 2, ROWS, 128), BF),
         ),
         in_specs=[vmem, vmem, vmem],
         out_specs=(vmem, vmem),
@@ -142,111 +187,183 @@
     )(m, w, v)
 
 
-def head_window(j, base):
-    first = (j // 2) * 128
-    return pl.ds(pl.multiple_of(first, 128), 256), base + j * HEAD_DIM - first
-
-
-def masked(ref, a, window, mask):
-    x = ref[:, a, :, window].reshape(1024, 256)
+def expand(dst, ref, a, half):
+    for b in range(4):
+        dst[b + half] = ref[:, a, b * 64 : b * 64 + 64].reshape(1024, 128)
+    shared = ref[:, a, 256:288].reshape(512, 128)
+    both = [x.reshape(16, 32, 128) for x in (shared, rolled(shared))]
+    dst[4 * (1 - half)] = jnp.concatenate(both, axis=1).reshape(1024, 128)
+
+
+def collapse(ref, a, src, half):
+    for b in range(4):
+        ref[:, a, b * 64 : b * 64 + 64] = src[b + half].reshape(16, 64, 128)
+    shared = src[4 * (1 - half)].reshape(16, 64, 128)
+    low, high = shared[:, :32].reshape(512, 128), shared[:, 32:].reshape(512, 128)
+    both = jnp.where(native(512, half), low, rolled(high))
+    ref[:, a, 256:288] = both.reshape(16, 32, 128)
+
+
+def head_window(j, half):
+    return j // 2, 64 * half + j * HEAD_DIM - (j // 2) * 128
+
+
+def tiles(ref, t, rows=slice(None)):
+    return jnp.concatenate([ref[t, rows], ref[t + 1, rows]], axis=1)
+
+
+def masked(x, mask):
     return jnp.where(mask, x, jnp.zeros_like(x))
 
 
-def probs_kernel(base_ref, qk_ref, p_ref, kh):
-    window, low = head_window(pl.program_id(0), base_ref[0])
-    kh[...] = masked(qk_ref, 1, window, lane_mask(1024, low))
+def put_tiles(ref, t, new, mask):
+    new = new.astype(BF)
+    for side in range(2):
+        lanes = slice(side * 128, side * 128 + 128)
+        ref[t + side] = jnp.where(mask[:, lanes], new[:, lanes], ref[t + side])
+
+
+def probs_kernel(half_ref, qk_ref, p_ref, q, k, kh):
+    half, j = half_ref[0], pl.program_id(0)
+
+    @pl.when(j == 0)
+    def _():
+        expand(q, qk_ref, 0, half)
+        expand(k, qk_ref, 1, half)
+
+    t, low = head_window(j, half)
+    kh[...] = masked(tiles(k, t), lane_mask(1024, low))
     for i in range(4):
         rows = slice(i * 256, (i + 1) * 256)
-        qb = qk_ref[4 * i : 4 * i + 4, 0, :, window].reshape(256, 256)
-        s = nt(kh[...], qb) * (SCALE * LOG2E)
+        s = nt(kh[...], tiles(q, t, rows)) * (SCALE * LOG2E)
         p = jnp.exp2(s - jnp.max(s, axis=0, keepdims=True))
         p_ref[0, :, rows] = (p * (1.0 / jnp.sum(p, axis=0, keepdims=True))).astype(BF)
 
 
-def probs(base, qk):
+def fixed(arrays):
+    return pl.BlockSpec((16, arrays, ROWS, 128), lambda j: (0, 0, 0, 0))
+
+
+SCALAR = pl.BlockSpec(memory_space=pltpu.SMEM)
+EACH_HEAD = pl.BlockSpec((1, 1024, 1024), lambda j: (j, 0, 0))
+TILES = pltpu.VMEM((5, 1024, 128), BF)
+WINDOW = pltpu.VMEM((1024, 256), BF)
+
+
+def probs(half, qk):
     return pl.pallas_call(
         probs_kernel,
         out_shape=jax.ShapeDtypeStruct((8, 1024, 1024), BF),
         grid=(8,),
-        in_specs=[
-            pl.BlockSpec(memory_space=pltpu.SMEM),
-            pl.BlockSpec((16, 2, 64, HALF), lambda j: (0, 0, 0, 0)),
-        ],
-        out_specs=pl.BlockSpec((1, 1024, 1024), lambda j: (j, 0, 0)),
-        scratch_shapes=[pltpu.VMEM((1024, 256), BF)],
+        in_specs=[SCALAR, fixed(2)],
+        out_specs=EACH_HEAD,
+        scratch_shapes=[TILES, TILES, WINDOW],
         compiler_params=pltpu.CompilerParams(vmem_limit_bytes=VMEM_LIMIT),
         cost_estimate=pl.CostEstimate(
             flops=20_000_000_000, bytes_accessed=20_000_000, transcendentals=8_400_000
         ),
         name="probs",
-    )(base, qk)
-
-
-def grads_kernel(base_ref, qk_ref, vg_ref, p_ref, out_ref, qh, kh, vh, gh, ds):
-    window, low = head_window(pl.program_id(0), base_ref[0])
+    )(half, qk)
+
+
+def value_kernel(half_ref, vg_ref, p_ref, out_ref, g, dv):
+    half, j = half_ref[0], pl.program_id(0)
+
+    @pl.when(j == 0)
+    def _():
+        expand(g, vg_ref, 1, half)
+
+    t, low = head_window(j, half)
+    put_tiles(dv, t, nn(p_ref[0], tiles(g, t)), lane_mask(1024, low))
+
+    @pl.when(j == 7)
+    def _():
+        collapse(out_ref, 0, dv, half)
+
+
+def value_grads(half, vg, p):
+    return pl.pallas_call(
+        value_kernel,
+        out_shape=jax.ShapeDtypeStruct((16, 1, ROWS, 128), BF),
+        grid=(8,),
+        in_specs=[SCALAR, fixed(2), EACH_HEAD],
+        out_specs=fixed(1),
+        scratch_shapes=[TILES, TILES],
+        compiler_params=pltpu.CompilerParams(vmem_limit_bytes=VMEM_LIMIT),
+        cost_estimate=pl.CostEstimate(
+            flops=5_000_000_000, bytes_accessed=20_000_000, transcendentals=0
+        ),
+        name="value_grads",
+    )(half, vg, p)
+
+
+def grads_kernel(half_ref, qk_ref, vg_ref, p_ref, out_ref, q, k, v, g, dq, dk, kh, vh, ds):
+    half, j = half_ref[0], pl.program_id(0)
+
+    @pl.when(j == 0)
+    def _():
+        for dst, ref, a in ((q, qk_ref, 0), (k, qk_ref, 1), (v, vg_ref, 0), (g, vg_ref, 1)):
+            expand(dst, ref, a, half)
+
+    t, low = head_window(j, half)
     mask = lane_mask(1024, low)
-    for dst, ref, a in ((qh, qk_ref, 0), (kh, qk_ref, 1), (vh, vg_ref, 0), (gh, vg_ref, 1)):
-        dst[...] = masked(ref, a, window, mask)
-    deep = mask.reshape(16, 64, 256)
-
-    def put(a, new):
-        new = new.astype(BF).reshape(16, 64, 256)
-        out_ref[:, a, :, window] = jnp.where(deep, new, out_ref[:, a, :, window])
-
+    kh[...] = tiles(k, t)
+    vh[...] = masked(tiles(v, t), mask)
     for i in range(4):
         rows = slice(i * 256, (i + 1) * 256)
-        dp = nt(vh[...], gh[rows])
+        dp = nt(vh[...], tiles(g, t, rows))
         p = p_ref[0, :, rows].astype(F32)
         delta = jnp.sum(p * dp, axis=0, keepdims=True)
         ds[:, rows] = (p * (dp - delta)).astype(BF)
-    put(2, nn(p_ref[0], gh[...]))
-    put(1, nn(ds[...], qh[...]) * SCALE)
-    put(0, tn(ds[...], kh[...]) * SCALE)
-
-
-def grads(base, qk, vg, p):
-    whole = pl.BlockSpec((16, 2, 64, HALF), lambda j: (0, 0, 0, 0))
+    put_tiles(dk, t, nn(ds[...], tiles(q, t)) * SCALE, mask)
+    put_tiles(dq, t, tn(ds[...], kh[...]) * SCALE, mask)
+
+    @pl.when(j == 7)
+    def _():
+        collapse(out_ref, 0, dq, half)
+        collapse(out_ref, 1, dk, half)
+
+
+def grads(half, qk, vg, p):
     return pl.pallas_call(
         grads_kernel,
-        out_shape=jax.ShapeDtypeStruct((16, 3, 64, HALF), BF),
+        out_shape=jax.ShapeDtypeStruct((16, 2, ROWS, 128), BF),
         grid=(8,),
-        in_specs=[
-            pl.BlockSpec(memory_space=pltpu.SMEM),
-            whole,
-            whole,
-            pl.BlockSpec((1, 1024, 1024), lambda j: (j, 0, 0)),
-        ],
-        out_specs=pl.BlockSpec((16, 3, 64, HALF), lambda j: (0, 0, 0, 0)),
-        scratch_shapes=[pltpu.VMEM((1024, 256), BF)] * 4 + [pltpu.VMEM((1024, 1024), BF)],
+        in_specs=[SCALAR, fixed(2), fixed(2), EACH_HEAD],
+        out_specs=fixed(2),
+        scratch_shapes=[TILES] * 6 + [WINDOW, WINDOW, pltpu.VMEM((1024, 1024), BF)],
         compiler_params=pltpu.CompilerParams(vmem_limit_bytes=VMEM_LIMIT),
         cost_estimate=pl.CostEstimate(
-            flops=22_000_000_000, bytes_accessed=26_000_000, transcendentals=0
+            flops=20_000_000_000, bytes_accessed=26_000_000, transcendentals=0
         ),
         name="grads",
-    )(base, qk, vg, p)
-
-
-def unpack_kernel(r_ref, *out_refs):
-    lane = lax.broadcasted_iota(jnp.int32, (8, 64, 128), 2)
-    for a, out in enumerate(out_refs):
-        out[:, :, :512] = r_ref[:, 0, a, :, :512]
-        out[:, :, 512:640] = jnp.where(
-            lane < 64, r_ref[:, 0, a, :, 512:640], r_ref[:, 1, a, :, :128]
-        )
-        out[:, :, 640:] = r_ref[:, 1, a, :, 128:]
-
-
-def unpack(r):
+    )(half, qk, vg, p)
+
+
+def unpack_kernel(qk_ref, v_ref, *out_refs):
+    for f in range(8):
+        for out, ref, a in zip(out_refs, (qk_ref, qk_ref, v_ref), (0, 1, 0)):
+            for half in range(2):
+                for b in range(4):
+                    lane = (b + 5 * half) * 128
+                    out[f, :, lane : lane + 128] = ref[f, half, a, b * 64 : b * 64 + 64]
+            first, second = ref[f, 0, a, 256:288], ref[f, 1, a, 256:288]
+            left = native(32, 0)
+            out[f, :32, 512:640] = jnp.where(left, first, second)
+            out[f, 32:, 512:640] = rolled(jnp.where(left, second, first))
+
+
+def unpack(qk, v):
     whole = jax.ShapeDtypeStruct((8, 64, D), BF)
     vmem = pl.BlockSpec(memory_space=pltpu.VMEM)
     return pl.pallas_call(
         unpack_kernel,
         out_shape=(whole,) * 3,
-        in_specs=[vmem],
+        in_specs=[vmem, vmem],
         out_specs=(vmem,) * 3,
         compiler_params=pltpu.CompilerParams(vmem_limit_bytes=32 * 1024 * 1024),
         name="unpack",
-    )(r)
+    )(qk, v)
 
 
 def exchange(x, axis):
@@ -257,23 +374,30 @@
     query_time, key_time, value_time, query_space, key_space, value_space, grad_output,
     outproj_time, queryproj_time, keyproj_time, valueproj_time, outproj_space,
 ):
-    base = (lax.axis_index("space") % 2 * 64).astype(jnp.int32).reshape(1)
+    half = (lax.axis_index("space") % 2).astype(jnp.int32).reshape(1)
+    qk = pack(query_space, key_space)
     t = jnp.stack([query_time, key_time, value_time, grad_output])
     t = t.reshape(4, 8, 8, 8, D).transpose(2, 0, 1, 3, 4).reshape(8, 4, 64, D)
+    t, qk = lax.optimization_barrier((t, qk))
     t = exchange(t, "tm")
-    qk = jnp.stack([query_space, key_space], axis=1)
-    qk = jnp.stack([qk[..., :HALF], qk[..., D - HALF :]], axis=1).reshape(16, 2, 64, HALF)
     qk, t = lax.optimization_barrier((qk, t))
-    qk = exchange(qk, "space")
+    qk = exchange(qk.reshape(16, 2, ROWS, 128), "space")
     middle = temporal(t, outproj_time, queryproj_time, keyproj_time, valueproj_time)
     middle, qk = lax.optimization_barrier((middle, qk))
     middle = exchange(middle, "tm")
     middle_grad, vg = project(middle, outproj_space, value_space)
     vg, qk = lax.optimization_barrier((vg, qk))
-    p = probs(base, qk)
-    vg = exchange(vg.reshape(16, 2, 64, HALF), "space")
-    out = exchange(grads(base, qk, vg, p), "space")
-    query_grad, key_grad, value_grad = unpack(out.reshape(8, 2, 3, 64, HALF))
+    p = probs(half, qk)
+    vg = exchange(vg.reshape(16, 2, ROWS, 128), "space")
+    dv = value_grads(half, vg, p)
+    dv, qk = lax.optimization_barrier((dv, qk))
+    out_v = exchange(dv, "space")
+    dqk = grads(half, qk, vg, p)
+    dqk, out_v = lax.optimization_barrier((dqk, out_v))
+    out_qk = exchange(dqk, "space")
+    query_grad, key_grad, value_grad = unpack(
+        out_qk.reshape(8, 2, 2, ROWS, 128), out_v.reshape(8, 2, 1, ROWS, 128)
+    )
     return query_grad, key_grad, value_grad, middle_grad
 
 

time: 285 us -> 265 us (0.930)
  waiting for transfers between devices: 69.3 us -> 11.9 us
  blocking collectives: 91.5 us -> 119 us
  Pallas kernels: 88.5 us -> 101 us
  other arithmetic: 6.34 us -> 0.69 us
    all_to_all x3, waiting for transfers between devices: 69.3 us -> 11.9 us  [exchange(): return lax.all_to_all(x, axis, 0, 0, tiled=True)]
    all_to_all x2 -> x3, blocking collectives: 91.5 us -> 119 us  [exchange(): return lax.all_to_all(x, axis, 0, 0, tiled=True)]
    pallas_call x2 -> x4, Pallas kernels: 29.1 us -> 40.3 us  [the longest x1 23.9 us: grads(): pl.pallas_call(grads_kernel, out_shape=jax.ShapeDtypeStruct((16, 2, ROWS,...]
    reshape x1, other arithmetic: 5.69 us -> 0.69 us  [per_device(): t = t.reshape(4, 8, 8, 8, D).transpose(2, 0, 1, 3, 4).reshape(8, 4, 64, D)]
    unnamed x8 -> x16, local copies, waits for them, and re-layouts: 1.53 us -> 5.31 us
  transfers between devices with their start and end apart: 3 -> 3, of which waited for: 3 -> 1; matrix products, arithmetic and copies ran while one was open for 1% -> 0% of each run, Pallas kernels for 19% -> 29%
where the time goes in v3:
time: 265 us
  blocking collectives  119 us (45%)
  Pallas kernels  101 us (38%)
  starting transfers between devices  25.8 us (10%)
  waiting for transfers between devices  11.9 us (4%)
  local copies, waits for them, and re-layouts  5.31 us (2%)
    all_to_all x3, blocking collectives, exchange(): return lax.all_to_all(x, axis, 0, 0, tiled=True)  119 us
    pallas_call x1, Pallas kernels, temporal(): pl.pallas_call(temporal_kernel, out_shape=jax.ShapeDtypeStruct((8, 64, D)...  34.3 us
    all_to_all x3, starting transfers between devices, exchange(): return lax.all_to_all(x, axis, 0, 0, tiled=True)  25.8 us
    pallas_call x1, Pallas kernels, grads(): pl.pallas_call(grads_kernel, out_shape=jax.ShapeDtypeStruct((16, 2, ROWS,...  23.9 us
    pallas_call x1, Pallas kernels, probs(): pl.pallas_call(probs_kernel, out_shape=jax.ShapeDtypeStruct((8, 1024, 102...  19.7 us
    pallas_call x1, Pallas kernels, value_grads(): pl.pallas_call(value_kernel, out_shape=jax.ShapeDtypeStruct((16, 1, ROWS,...  12.5 us
    all_to_all x3, waiting for transfers between devices, exchange(): return lax.all_to_all(x, axis, 0, 0, tiled=True)  11.9 us
    pallas_call x1, Pallas kernels, project(): pl.pallas_call(project_kernel, out_shape=(jax.ShapeDtypeStruct((8, 64, D)...  6.47 us
  transfers between devices with their start and end apart: 3, of which 1 were waited for; matrix products, arithmetic and copies ran while one was open for 0% of the time, Pallas kernels for 29%

profile of v3, /device:TPU:1, one launch (start us, length us, event | category | flops | bytes accessed | tf_op | source)
XLA Modules:
  0.0 264.6 jit_solution(15213010862792798076)
XLA Ops:
  0.6 0.0 copy-start
  0.6 1.3 copy-done
  1.9 0.0 copy-start.1
  1.9 1.3 copy-done.1
  3.2 0.0 copy-start.4
  3.2 0.0 copy-start.5
  3.2 0.0 copy-start.6
  3.2 0.0 copy-start.7
  3.2 1.8 pack.1
  5.0 0.0 copy-done.4
  5.0 0.5 copy-done.5
  5.6 0.4 copy-done.6
  6.0 0.4 copy-done.7
  6.4 0.7 copy_bitcast_fusion
  7.1 59.9 %all_to_all.30.r_ref = bf16[8,4,64,1152]{3,2,1,0:T(8,128)(2,1)} all-to-all(bf16[8,4,64,1152]{3,2,1,0:T(8,128)(2,1)S(1)} %copy_bitcast_fusion), channel_id=1, replica_groups=mesh['tm'=8,'space'=16] {'tm'}, dimensions={0} | all-to-all | bytes 9437184 | tf_op jit(solution)/shard_map/all_to_all | solution.py:370
  66.9 9.8 %all-to-all-start.1 = ((bf16[16,2,288,128]{3,2,1,0:T(8,128)(2,1)}), bf16[16,2,288,128]{3,2,1,0:T(8,128)(2,1)S(1)}, u32[]{:S(2)}, u32[]{:S(2)}) async-start(bf16[16,2,288,128]{3,2,1,0:T(8,128)(2,1)} %bitcast.7), calls=%async_computation.1 | async-start | bytes 4718592 | tf_op jit(solution)/shard_map/all_to_all | solution.py:370
  76.8 34.3 %temporal.1 = bf16[8,64,1152]{2,1,0:T(8,128)(2,1)} custom-call(bf16[8,4,64,1152]{3,2,1,0:T(8,128)(2,1)} %all_to_all.30.r_ref, bf16[1152,1152]{1,0:T(8,128)(2,1)} %wo_hbm.1, bf16[1152,1152]{1,0:T(8,128)(2,1)} %wq_hbm.1, bf16[1152,1152]{1,0:T(8,128)(2,1)} %wk_hbm.1, bf16[1152,1152]{1,0:T(8,128)(2,1)} %wv_hbm.1), custom_call_target="tpu_custom_call" | custom-call | flops 20000000000 | bytes 16000000 | tf_op jit(solution)/shard_map/temporal/pallas_call | solution.py:100
  111.0 0.0 all-to-all-done.1.qk_ref
  111.1 0.0 copy-start.3
  111.1 21.2 %all_to_all.31.m_ref = bf16[8,64,1152]{2,1,0:T(8,128)(2,1)} all-to-all(bf16[8,64,1152]{2,1,0:T(8,128)(2,1)} %temporal.1), channel_id=1, replica_groups=mesh['tm'=8,'space'=16] {'tm'}, dimensions={0} | all-to-all | bytes 2359296 | tf_op jit(solution)/shard_map/all_to_all | solution.py:370
  132.3 6.5 %project.1 = (bf16[8,64,1152]{2,1,0:T(8,128)(2,1)}, bf16[8,2,2,288,128]{4,3,2,1,0:T(8,128)(2,1)}) custom-call(bf16[8,64,1152]{2,1,0:T(8,128)(2,1)} %all_to_all.31.m_ref, bf16[1152,1152]{1,0:T(8,128)(2,1)} %w_ref.1, bf16[8,64,1152]{2,1,0:T(8,128)(2,1)} %v_ref.1), custom_call_target="tpu_custom_call" | custom-call | flops 4000000000 | bytes 8000000 | tf_op jit(solution)/shard_map/project/pallas_call | solution.py:174
  138.7 0.0 copy-done.3
  138.7 8.0 %all-to-all-start.3 = ((bf16[16,2,288,128]{3,2,1,0:T(8,128)(2,1)}), bf16[16,2,288,128]{3,2,1,0:T(8,128)(2,1)S(1)}, u32[]{:S(2)}, u32[]{:S(2)}) async-start(bf16[16,2,288,128]{3,2,1,0:T(8,128)(2,1)} %bitcast.15), calls=%async_computation.3 | async-start | bytes 4718592 | tf_op jit(solution)/shard_map/all_to_all | solution.py:370
  146.7 19.7 %probs.1.p_ref = bf16[8,1024,1024]{2,1,0:T(8,128)(2,1)} custom-call(s32[1]{0:T(128)} %bitcast.half_ref, bf16[16,2,288,128]{3,2,1,0:T(8,128)(2,1)} %copy-done.3), custom_call_target="tpu_custom_call" | custom-call | flops 20000000000 | bytes 20000000 | tf_op jit(solution)/shard_map/probs/pallas_call | solution.py:254
  166.4 11.9 %all-to-all-done.3.vg_ref = bf16[16,2,288,128]{3,2,1,0:T(8,128)(2,1)S(1)} async-done(((bf16[16,2,288,128]{3,2,1,0:T(8,128)(2,1)}), bf16[16,2,288,128]{3,2,1,0:T(8,128)(2,1)S(1)}, u32[]{:S(2)}, u32[]{:S(2)}) %all-to-all-start.3) | async-done | bytes 2359328 | tf_op jit(solution)/shard_map/all_to_all | solution.py:370
  178.3 0.0 copy-start.2
  178.3 1.4 copy-done.2
  179.8 12.5 %value_grads.1 = bf16[16,1,288,128]{3,2,1,0:T(8,128)(2,1)} custom-call(s32[1]{0:T(128)} %bitcast.half_ref, bf16[16,2,288,128]{3,2,1,0:T(8,128)(2,1)} %copy-done.2, bf16[8,1024,1024]{2,1,0:T(8,128)(2,1)} %probs.1.p_ref), custom_call_target="tpu_custom_call" | custom-call | flops 5000000000 | bytes 20000000 | tf_op jit(solution)/shard_map/value_grads/pallas_call | solution.py:285
  192.2 8.0 %all-to-all-start.4 = ((bf16[16,1,288,128]{3,2,1,0:T(8,128)(2,1)}), bf16[16,1,288,128]{3,2,1,0:T(8,128)(2,1)S(1)}, u32[]{:S(2)}, u32[]{:S(2)}) async-start(bf16[16,1,288,128]{3,2,1,0:T(8,128)(2,1)} %value_grads.1), calls=%async_computation.4 | async-start | bytes 2359296 | tf_op jit(solution)/shard_map/all_to_all | solution.py:370
  200.2 23.9 %grads.1 = bf16[16,2,288,128]{3,2,1,0:T(8,128)(2,1)} custom-call(s32[1]{0:T(128)} %bitcast.half_ref, bf16[16,2,288,128]{3,2,1,0:T(8,128)(2,1)} %copy-done.3, bf16[16,2,288,128]{3,2,1,0:T(8,128)(2,1)} %copy-done.2, bf16[8,1024,1024]{2,1,0:T(8,128)(2,1)} %probs.1.p_ref), custom_call_target="tpu_custom_call" | custom-call | flops 20000000000 | bytes 26000000 | tf_op jit(solution)/shard_map/grads/pallas_call | solution.py:328
  224.2 0.0 all-to-all-done.4
  224.2 38.4 %all_to_all.32 = bf16[16,2,288,128]{3,2,1,0:T(8,128)(2,1)S(1)} all-to-all(bf16[16,2,288,128]{3,2,1,0:T(8,128)(2,1)} %grads.1), channel_id=1, replica_groups=mesh['tm'=8,'space'=16] {'space'}, dimensions={0} | all-to-all | bytes 4718592 | tf_op jit(solution)/shard_map/all_to_all | solution.py:370
  262.6 2.0 unpack.1
Async XLA Ops:
  0.6 1.3 copy-start
  1.9 1.3 copy-start.1
  3.2 1.8 copy-start.4
  3.2 2.4 copy-start.5
  3.2 2.8 %copy-start.6 = (bf16[8,64,1152]{2,1,0:T(8,128)(2,1)S(1)}, bf16[8,64,1152]{2,1,0:T(8,128)(2,1)}, u32[]{:S(2)}) copy-start(bf16[8,64,1152]{2,1,0:T(8,128)(2,1)} %param.13) | copy-start | bytes 3538948
  3.2 3.2 %copy-start.7 = (bf16[8,64,1152]{2,1,0:T(8,128)(2,1)S(1)}, bf16[8,64,1152]{2,1,0:T(8,128)(2,1)}, u32[]{:S(2)}) copy-start(bf16[8,64,1152]{2,1,0:T(8,128)(2,1)} %param.12) | copy-start | bytes 3538948
  66.9 44.1 %all-to-all-start.1 = ((bf16[16,2,288,128]{3,2,1,0:T(8,128)(2,1)}), bf16[16,2,288,128]{3,2,1,0:T(8,128)(2,1)S(1)}, u32[]{:S(2)}, u32[]{:S(2)}) async-start(bf16[16,2,288,128]{3,2,1,0:T(8,128)(2,1)} %bitcast.7), calls=%async_computation.1 | async-start | bytes 4718592 | tf_op jit(solution)/shard_map/all_to_all | solution.py:370
  111.1 27.7 %copy-start.3 = (bf16[16,2,288,128]{3,2,1,0:T(8,128)(2,1)}, bf16[16,2,288,128]{3,2,1,0:T(8,128)(2,1)S(1)}, u32[]{:S(2)}) copy-start(bf16[16,2,288,128]{3,2,1,0:T(8,128)(2,1)S(1)} %all-to-all-done.1.qk_ref) | copy-start | bytes 7077892
  138.7 39.6 %all-to-all-start.3 = ((bf16[16,2,288,128]{3,2,1,0:T(8,128)(2,1)}), bf16[16,2,288,128]{3,2,1,0:T(8,128)(2,1)S(1)}, u32[]{:S(2)}, u32[]{:S(2)}) async-start(bf16[16,2,288,128]{3,2,1,0:T(8,128)(2,1)} %bitcast.15), calls=%async_computation.3 | async-start | bytes 4718592 | tf_op jit(solution)/shard_map/all_to_all | solution.py:370
  178.3 1.4 copy-start.2
  192.2 32.0 %all-to-all-start.4 = ((bf16[16,1,288,128]{3,2,1,0:T(8,128)(2,1)}), bf16[16,1,288,128]{3,2,1,0:T(8,128)(2,1)S(1)}, u32[]{:S(2)}, u32[]{:S(2)}) async-start(bf16[16,1,288,128]{3,2,1,0:T(8,128)(2,1)} %value_grads.1), calls=%async_computation.4 | async-start | bytes 2359296 | tf_op jit(solution)/shard_map/all_to_all | solution.py:370

commit v4 on v3

--- a/solution.py
+++ b/solution.py
@@ -54,33 +54,43 @@
         dst[...] = nn(to_patch, r_ref[:, a].reshape(512, D)).astype(BF)
     copies[0].wait()
     g[...] = nt(g0[...], wo[...]).astype(BF)
-    m_patch = lax.broadcasted_iota(jnp.int32, (128, 128), 0) // 64
-    l_patch = lax.broadcasted_iota(jnp.int32, (128, 128), 1) // 64
-    same = m_patch == l_patch
-
-    def head(h, carry):
-        first = jnp.minimum(h * HEAD_DIM // 128, D // 128 - 2) * 128
+    same = (
+        lax.broadcasted_iota(jnp.int32, (2, 128, 128), 1) // 64
+        == lax.broadcasted_iota(jnp.int32, (2, 128, 128), 2) // 64
+    )
+
+    def pair(i, carry):
+        first = i * 2 * HEAD_DIM // 128 * 128
         window = pl.ds(pl.multiple_of(first, 128), 256)
-        mask = lane_mask(128, h * HEAD_DIM - first)
+        low = i * 2 * HEAD_DIM - first
+        masks = [lane_mask(128, low), lane_mask(128, low + HEAD_DIM)]
+        either = masks[0] | masks[1]
+
+        def stacked(x):
+            return jnp.concatenate([jnp.where(mask, x, jnp.zeros_like(x)) for mask in masks])
+
+        def beside(x):
+            return jnp.concatenate([x[0], x[1]], axis=1)
+
         for b in range(4):
             rows = pl.ds(b * 128, 128)
             qb, kb, vb, gb = [ref[rows, window] for ref in (q, k, v, g)]
-            kh = jnp.where(mask, kb, jnp.zeros_like(kb))
-            vh = jnp.where(mask, vb, jnp.zeros_like(vb))
-            s = jnp.where(same, nt(kh, qb) * (SCALE * LOG2E), -1e30)
-            p = jnp.exp2(s - jnp.max(s, axis=0, keepdims=True))
-            p = p * (1.0 / jnp.sum(p, axis=0, keepdims=True))
-            dp = nt(vh, gb)
-            delta = jnp.sum(p * dp, axis=0, keepdims=True)
+            kh = stacked(kb)
+            s = nt(kh, qb).reshape(2, 128, 128) * (SCALE * LOG2E)
+            s = jnp.where(same, s, -1e30)
+            p = jnp.exp2(s - jnp.max(s, axis=1, keepdims=True))
+            p = p * (1.0 / jnp.sum(p, axis=1, keepdims=True))
+            dp = nt(stacked(vb), gb).reshape(2, 128, 128)
+            delta = jnp.sum(p * dp, axis=1, keepdims=True)
             ds = (p * (dp - delta)).astype(BF)
-            new_dk = (nn(ds, qb) * SCALE).astype(BF)
-            new_dv = nn(p.astype(BF), gb).astype(BF)
-            new_dq = (tn(ds, kb) * SCALE).astype(BF)
+            new_dk = (nn(beside(ds), stacked(qb)) * SCALE).astype(BF)
+            new_dv = nn(beside(p.astype(BF)), stacked(gb)).astype(BF)
+            new_dq = (tn(ds.reshape(256, 128), kh) * SCALE).astype(BF)
             for ref, new in ((dq, new_dq), (dk, new_dk), (dv, new_dv)):
-                ref[rows, window] = jnp.where(mask, new, ref[rows, window])
+                ref[rows, window] = jnp.where(either, new, ref[rows, window])
         return carry
 
-    lax.fori_loop(0, D // HEAD_DIM, head, 0)
+    lax.fori_loop(0, D // HEAD_DIM // 2, pair, 0)
     for copy in copies[1:]:
         copy.wait()
     middle = (
@@ -179,7 +189,7 @@
         ),
         in_specs=[vmem, vmem, vmem],
         out_specs=(vmem, vmem),
-        compiler_params=pltpu.CompilerParams(vmem_limit_bytes=VMEM_LIMIT),
+        compiler_params=pltpu.CompilerParams(vmem_limit_bytes=32 * 1024 * 1024),
         cost_estimate=pl.CostEstimate(
             flops=4_000_000_000, bytes_accessed=8_000_000, transcendentals=0
         ),
@@ -240,14 +250,15 @@
         p_ref[0, :, rows] = (p * (1.0 / jnp.sum(p, axis=0, keepdims=True))).astype(BF)
 
 
+SCALAR = pl.BlockSpec(memory_space=pltpu.SMEM)
+VMEM = pl.BlockSpec(memory_space=pltpu.VMEM)
+TILES = pltpu.VMEM((5, 1024, 128), BF)
+WINDOW = pltpu.VMEM((1024, 256), BF)
+EACH_HEAD = pl.BlockSpec((1, 1024, 1024), lambda j: (j, 0, 0))
+
+
 def fixed(arrays):
     return pl.BlockSpec((16, arrays, ROWS, 128), lambda j: (0, 0, 0, 0))
-
-
-SCALAR = pl.BlockSpec(memory_space=pltpu.SMEM)
-EACH_HEAD = pl.BlockSpec((1, 1024, 1024), lambda j: (j, 0, 0))
-TILES = pltpu.VMEM((5, 1024, 128), BF)
-WINDOW = pltpu.VMEM((1024, 256), BF)
 
 
 def probs(half, qk):
@@ -266,38 +277,9 @@
     )(half, qk)
 
 
-def value_kernel(half_ref, vg_ref, p_ref, out_ref, g, dv):
-    half, j = half_ref[0], pl.program_id(0)
-
-    @pl.when(j == 0)
-    def _():
-        expand(g, vg_ref, 1, half)
-
-    t, low = head_window(j, half)
-    put_tiles(dv, t, nn(p_ref[0], tiles(g, t)), lane_mask(1024, low))
-
-    @pl.when(j == 7)
-    def _():
-        collapse(out_ref, 0, dv, half)
-
-
-def value_grads(half, vg, p):
-    return pl.pallas_call(
-        value_kernel,
-        out_shape=jax.ShapeDtypeStruct((16, 1, ROWS, 128), BF),
-        grid=(8,),
-        in_specs=[SCALAR, fixed(2), EACH_HEAD],
-        out_specs=fixed(1),
-        scratch_shapes=[TILES, TILES],
-        compiler_params=pltpu.CompilerParams(vmem_limit_bytes=VMEM_LIMIT),
-        cost_estimate=pl.CostEstimate(
-            flops=5_000_000_000, bytes_accessed=20_000_000, transcendentals=0
-        ),
-        name="value_grads",
-    )(half, vg, p)
-
-
-def grads_kernel(half_ref, qk_ref, vg_ref, p_ref, out_ref, q, k, v, g, dq, dk, kh, vh, ds):
+def grads_kernel(
+    half_ref, qk_ref, vg_ref, p_ref, out_ref, q, k, v, g, dq, dk, dv, kh, vh, ds
+):
     half, j = half_ref[0], pl.program_id(0)
 
     @pl.when(j == 0)
@@ -315,55 +297,56 @@
         p = p_ref[0, :, rows].astype(F32)
         delta = jnp.sum(p * dp, axis=0, keepdims=True)
         ds[:, rows] = (p * (dp - delta)).astype(BF)
+    put_tiles(dv, t, nn(p_ref[0], tiles(g, t)), mask)
     put_tiles(dk, t, nn(ds[...], tiles(q, t)) * SCALE, mask)
     put_tiles(dq, t, tn(ds[...], kh[...]) * SCALE, mask)
 
     @pl.when(j == 7)
     def _():
-        collapse(out_ref, 0, dq, half)
-        collapse(out_ref, 1, dk, half)
+        for a, src in enumerate((dq, dk, dv)):
+            collapse(out_ref, a, src, half)
 
 
 def grads(half, qk, vg, p):
     return pl.pallas_call(
         grads_kernel,
-        out_shape=jax.ShapeDtypeStruct((16, 2, ROWS, 128), BF),
+        out_shape=jax.ShapeDtypeStruct((16, 3, ROWS, 128), BF),
         grid=(8,),
         in_specs=[SCALAR, fixed(2), fixed(2), EACH_HEAD],
-        out_specs=fixed(2),
-        scratch_shapes=[TILES] * 6 + [WINDOW, WINDOW, pltpu.VMEM((1024, 1024), BF)],
+        out_specs=fixed(3),
+        scratch_shapes=[TILES] * 7 + [WINDOW, WINDOW, pltpu.VMEM((1024, 1024), BF)],
         compiler_params=pltpu.CompilerParams(vmem_limit_bytes=VMEM_LIMIT),
         cost_estimate=pl.CostEstimate(
-            flops=20_000_000_000, bytes_accessed=26_000_000, transcendentals=0
+            flops=25_000_000_000, bytes_accessed=26_000_000, transcendentals=0
         ),
         name="grads",
     )(half, qk, vg, p)
 
 
-def unpack_kernel(qk_ref, v_ref, *out_refs):
+def unpack_kernel(r_ref, *out_refs):
     for f in range(8):
-        for out, ref, a in zip(out_refs, (qk_ref, qk_ref, v_ref), (0, 1, 0)):
+        for a, out in enumerate(out_refs):
             for half in range(2):
                 for b in range(4):
                     lane = (b + 5 * half) * 128
-                    out[f, :, lane : lane + 128] = ref[f, half, a, b * 64 : b * 64 + 64]
-            first, second = ref[f, 0, a, 256:288], ref[f, 1, a, 256:288]
+                    out[f, :, lane : lane + 128] = r_ref[f, half, a, b * 64 : b * 64 + 64]
+            first, second = r_ref[f, 0, a, 256:288], r_ref[f, 1, a, 256:288]
             left = native(32, 0)
             out[f, :32, 512:640] = jnp.where(left, first, second)
             out[f, 32:, 512:640] = rolled(jnp.where(left, second, first))
 
 
-def unpack(qk, v):
+def unpack(r):
     whole = jax.ShapeDtypeStruct((8, 64, D), BF)
     vmem = pl.BlockSpec(memory_space=pltpu.VMEM)
     return pl.pallas_call(
         unpack_kernel,
         out_shape=(whole,) * 3,
-        in_specs=[vmem, vmem],
+        in_specs=[vmem],
         out_specs=(vmem,) * 3,
         compiler_params=pltpu.CompilerParams(vmem_limit_bytes=32 * 1024 * 1024),
         name="unpack",
-    )(qk, v)
+    )(r)
 
 
 def exchange(x, axis):
@@ -389,15 +372,8 @@
     vg, qk = lax.optimization_barrier((vg, qk))
     p = probs(half, qk)
     vg = exchange(vg.reshape(16, 2, ROWS, 128), "space")
-    dv = value_grads(half, vg, p)
-    dv, qk = lax.optimization_barrier((dv, qk))
-    out_v = exchange(dv, "space")
-    dqk = grads(half, qk, vg, p)
-    dqk, out_v = lax.optimization_barrier((dqk, out_v))
-    out_qk = exchange(dqk, "space")
-    query_grad, key_grad, value_grad = unpack(
-        out_qk.reshape(8, 2, 2, ROWS, 128), out_v.reshape(8, 2, 1, ROWS, 128)
-    )
+    out = exchange(grads(half, qk, vg, p), "space")
+    query_grad, key_grad, value_grad = unpack(out.reshape(8, 2, 3, ROWS, 128))
     return query_grad, key_grad, value_grad, middle_grad
 
 

time: 265 us -> 256 us (0.966)
  Pallas kernels: 101 us -> 80.7 us
  blocking collectives: 119 us -> 132 us
  starting transfers between devices: 25.8 us -> 19.2 us
  waiting for transfers between devices: 11.9 us -> 17.9 us
    all_to_all x3, blocking collectives: 119 us -> 132 us  [exchange(): return lax.all_to_all(x, axis, 0, 0, tiled=True)]
    pallas_call x3 -> x2, Pallas kernels: 38.5 us -> 29.3 us  [the longest x1 27.3 us: grads(): pl.pallas_call(grads_kernel, out_shape=jax.ShapeDtypeStruct((16, 3, ROWS,...]
    pallas_call x1, Pallas kernels: 34.3 us -> 25.8 us  [temporal(): pl.pallas_call(temporal_kernel, out_shape=jax.ShapeDtypeStruct((8, 64, D)...]
    all_to_all x3 -> x2, starting transfers between devices: 25.8 us -> 19.2 us  [exchange(): return lax.all_to_all(x, axis, 0, 0, tiled=True)]
    all_to_all x3 -> x2, waiting for transfers between devices: 11.9 us -> 17.9 us  [exchange(): return lax.all_to_all(x, axis, 0, 0, tiled=True)]
    unnamed x16 -> x18, local copies, waits for them, and re-layouts: 5.31 us -> 5.32 us
  transfers between devices with their start and end apart: 3 -> 2, of which waited for: 1 -> 2; matrix products, arithmetic and copies ran while one was open for 0% -> 0% of each run, Pallas kernels for 29% -> 18%
where the time goes in v4:
time: 256 us
  blocking collectives  132 us (52%)
  Pallas kernels  80.7 us (32%)
  starting transfers between devices  19.2 us (8%)
  waiting for transfers between devices  17.9 us (7%)
  local copies, waits for them, and re-layouts  5.32 us (2%)
    all_to_all x3, blocking collectives, exchange(): return lax.all_to_all(x, axis, 0, 0, tiled=True)  132 us
    pallas_call x1, Pallas kernels, grads(): pl.pallas_call(grads_kernel, out_shape=jax.ShapeDtypeStruct((16, 3, ROWS,...  27.3 us
    pallas_call x1, Pallas kernels, temporal(): pl.pallas_call(temporal_kernel, out_shape=jax.ShapeDtypeStruct((8, 64, D)...  25.8 us
    pallas_call x1, Pallas kernels, probs(): pl.pallas_call(probs_kernel, out_shape=jax.ShapeDtypeStruct((8, 1024, 102...  19.7 us
    all_to_all x2, starting transfers between devices, exchange(): return lax.all_to_all(x, axis, 0, 0, tiled=True)  19.2 us
    all_to_all x2, waiting for transfers between devices, exchange(): return lax.all_to_all(x, axis, 0, 0, tiled=True)  17.9 us
    unnamed x18, local copies, waits for them, and re-layouts  5.32 us
  transfers between devices with their start and end apart: 2, of which 2 were waited for; matrix products, arithmetic and copies ran while one was open for 0% of the time, Pallas kernels for 18%

profile of v4, /device:TPU:1, one launch (start us, length us, event | category | flops | bytes accessed | tf_op | source)
XLA Modules:
  0.0 256.0 jit_solution(4837646373506953040)
XLA Ops:
  0.6 0.0 copy-start
  0.6 1.3 copy-done
  1.9 0.0 copy-start.1
  1.9 1.3 copy-done.1
  3.2 0.0 copy-start.5
  3.2 0.0 copy-start.6
  3.2 0.0 copy-start.7
  3.2 0.0 copy-start.8
  3.2 1.8 pack.1
  5.0 0.0 copy-done.5
  5.0 0.5 copy-done.6
  5.6 0.4 copy-done.7
  6.0 0.4 copy-done.8
  6.4 0.7 copy_bitcast_fusion
  7.1 59.9 %all_to_all.25.r_ref = bf16[8,4,64,1152]{3,2,1,0:T(8,128)(2,1)} all-to-all(bf16[8,4,64,1152]{3,2,1,0:T(8,128)(2,1)S(1)} %copy_bitcast_fusion), channel_id=1, replica_groups=mesh['tm'=8,'space'=16] {'tm'}, dimensions={0} | all-to-all | bytes 9437184 | tf_op jit(solution)/shard_map/all_to_all | solution.py:353
  66.9 9.8 %all-to-all-start.1 = ((bf16[16,2,288,128]{3,2,1,0:T(8,128)(2,1)}), bf16[16,2,288,128]{3,2,1,0:T(8,128)(2,1)}, u32[]{:S(2)}, u32[]{:S(2)}) async-start(bf16[16,2,288,128]{3,2,1,0:T(8,128)(2,1)} %bitcast.7), calls=%async_computation.1 | async-start | bytes 4718592 | tf_op jit(solution)/shard_map/all_to_all | solution.py:353
  76.8 0.0 copy-start.2
  76.8 25.8 %temporal.1 = bf16[8,64,1152]{2,1,0:T(8,128)(2,1)} custom-call(bf16[8,4,64,1152]{3,2,1,0:T(8,128)(2,1)} %all_to_all.25.r_ref, bf16[1152,1152]{1,0:T(8,128)(2,1)} %wo_hbm.1, bf16[1152,1152]{1,0:T(8,128)(2,1)} %wq_hbm.1, bf16[1152,1152]{1,0:T(8,128)(2,1)} %wk_hbm.1, bf16[1152,1152]{1,0:T(8,128)(2,1)} %wv_hbm.1), custom_call_target="tpu_custom_call" | custom-call | flops 20000000000 | bytes 16000000 | tf_op jit(solution)/shard_map/temporal/pallas_call | solution.py:110
  102.6 5.9 %all-to-all-done.1.qk_ref = bf16[16,2,288,128]{3,2,1,0:T(8,128)(2,1)} async-done(((bf16[16,2,288,128]{3,2,1,0:T(8,128)(2,1)}), bf16[16,2,288,128]{3,2,1,0:T(8,128)(2,1)}, u32[]{:S(2)}, u32[]{:S(2)}) %all-to-all-start.1) | async-done | bytes 2359328 | tf_op jit(solution)/shard_map/all_to_all | solution.py:353
  108.5 0.0 copy-start.3
  108.5 20.1 %all_to_all.26.m_ref = bf16[8,64,1152]{2,1,0:T(8,128)(2,1)S(1)} all-to-all(bf16[8,64,1152]{2,1,0:T(8,128)(2,1)} %temporal.1), channel_id=1, replica_groups=mesh['tm'=8,'space'=16] {'tm'}, dimensions={0} | all-to-all | bytes 2359296 | tf_op jit(solution)/shard_map/all_to_all | solution.py:353
  128.6 0.0 copy-done.2
  128.6 0.0 copy-done.3
  128.6 4.1 %project.1 = (bf16[8,64,1152]{2,1,0:T(8,128)(2,1)}, bf16[8,2,2,288,128]{4,3,2,1,0:T(8,128)(2,1)}) custom-call(bf16[8,64,1152]{2,1,0:T(8,128)(2,1)S(1)} %all_to_all.26.m_ref, bf16[1152,1152]{1,0:T(8,128)(2,1)S(1)} %copy-done.2, bf16[8,64,1152]{2,1,0:T(8,128)(2,1)S(1)} %copy-done.3), custom_call_target="tpu_custom_call" | custom-call | flops 4000000000 | bytes 8000000 | tf_op jit(solution)/shard_map/project/pallas_call | solution.py:184
  132.6 9.4 %all-to-all-start.3 = ((bf16[16,2,288,128]{3,2,1,0:T(8,128)(2,1)}), bf16[16,2,288,128]{3,2,1,0:T(8,128)(2,1)S(1)}, u32[]{:S(2)}, u32[]{:S(2)}) async-start(bf16[16,2,288,128]{3,2,1,0:T(8,128)(2,1)} %bitcast.8), calls=%async_computation.3 | async-start | bytes 4718592 | tf_op jit(solution)/shard_map/all_to_all | solution.py:353
  142.0 19.7 %probs.1.p_ref = bf16[8,1024,1024]{2,1,0:T(8,128)(2,1)} custom-call(s32[1]{0:T(128)} %bitcast.half_ref, bf16[16,2,288,128]{3,2,1,0:T(8,128)(2,1)} %all-to-all-done.1.qk_ref), custom_call_target="tpu_custom_call" | custom-call | flops 20000000000 | bytes 20000000 | tf_op jit(solution)/shard_map/probs/pallas_call | solution.py:265
  161.7 11.9 %all-to-all-done.3.vg_ref = bf16[16,2,288,128]{3,2,1,0:T(8,128)(2,1)S(1)} async-done(((bf16[16,2,288,128]{3,2,1,0:T(8,128)(2,1)}), bf16[16,2,288,128]{3,2,1,0:T(8,128)(2,1)S(1)}, u32[]{:S(2)}, u32[]{:S(2)}) %all-to-all-start.3) | async-done | bytes 2359328 | tf_op jit(solution)/shard_map/all_to_all | solution.py:353
  173.6 0.0 copy-start.4
  173.7 1.4 copy-done.4
  175.1 27.3 %grads.1 = bf16[16,3,288,128]{3,2,1,0:T(8,128)(2,1)} custom-call(s32[1]{0:T(128)} %bitcast.half_ref, bf16[16,2,288,128]{3,2,1,0:T(8,128)(2,1)} %all-to-all-done.1.qk_ref, bf16[16,2,288,128]{3,2,1,0:T(8,128)(2,1)} %copy-done.4, bf16[8,1024,1024]{2,1,0:T(8,128)(2,1)} %probs.1.p_ref), custom_call_target="tpu_custom_call" | custom-call | flops 24999999488 | bytes 26000000 | tf_op jit(solution)/shard_map/grads/pallas_call | solution.py:311
  202.4 51.6 %all_to_all.27 = bf16[16,3,288,128]{3,2,1,0:T(8,128)(2,1)S(1)} all-to-all(bf16[16,3,288,128]{3,2,1,0:T(8,128)(2,1)} %grads.1), channel_id=1, replica_groups=mesh['tm'=8,'space'=16] {'space'}, dimensions={0} | all-to-all | bytes 7077888 | tf_op jit(solution)/shard_map/all_to_all | solution.py:353
  254.0 2.0 unpack.1
Async XLA Ops:
  0.6 1.3 copy-start
  1.9 1.3 copy-start.1
  3.2 1.8 copy-start.5
  3.2 2.4 copy-start.6
  3.2 2.8 %copy-start.7 = (bf16[8,64,1152]{2,1,0:T(8,128)(2,1)S(1)}, bf16[8,64,1152]{2,1,0:T(8,128)(2,1)}, u32[]{:S(2)}) copy-start(bf16[8,64,1152]{2,1,0:T(8,128)(2,1)} %param.13) | copy-start | bytes 3538948
  3.2 3.2 %copy-start.8 = (bf16[8,64,1152]{2,1,0:T(8,128)(2,1)S(1)}, bf16[8,64,1152]{2,1,0:T(8,128)(2,1)}, u32[]{:S(2)}) copy-start(bf16[8,64,1152]{2,1,0:T(8,128)(2,1)} %param.12) | copy-start | bytes 3538948
  66.9 41.6 %all-to-all-start.1 = ((bf16[16,2,288,128]{3,2,1,0:T(8,128)(2,1)}), bf16[16,2,288,128]{3,2,1,0:T(8,128)(2,1)}, u32[]{:S(2)}, u32[]{:S(2)}) async-start(bf16[16,2,288,128]{3,2,1,0:T(8,128)(2,1)} %bitcast.7), calls=%async_computation.1 | async-start | bytes 4718592 | tf_op jit(solution)/shard_map/all_to_all | solution.py:353
  76.8 51.8 %copy-start.2 = (bf16[1152,1152]{1,0:T(8,128)(2,1)S(1)}, bf16[1152,1152]{1,0:T(8,128)(2,1)}, u32[]{:S(2)}) copy-start(bf16[1152,1152]{1,0:T(8,128)(2,1)} %w_ref.1) | copy-start | bytes 7962628
  108.5 20.1 %copy-start.3 = (bf16[8,64,1152]{2,1,0:T(8,128)(2,1)S(1)}, bf16[8,64,1152]{2,1,0:T(8,128)(2,1)}, u32[]{:S(2)}) copy-start(bf16[8,64,1152]{2,1,0:T(8,128)(2,1)} %v_ref.1) | copy-start | bytes 3538948
  132.6 41.0 %all-to-all-start.3 = ((bf16[16,2,288,128]{3,2,1,0:T(8,128)(2,1)}), bf16[16,2,288,128]{3,2,1,0:T(8,128)(2,1)S(1)}, u32[]{:S(2)}, u32[]{:S(2)}) async-start(bf16[16,2,288,128]{3,2,1,0:T(8,128)(2,1)} %bitcast.8), calls=%async_computation.3 | async-start | bytes 4718592 | tf_op jit(solution)/shard_map/all_to_all | solution.py:353
  173.6 1.4 copy-start.4

commit v5 on v4

--- a/solution.py
+++ b/solution.py
@@ -257,19 +257,15 @@
 EACH_HEAD = pl.BlockSpec((1, 1024, 1024), lambda j: (j, 0, 0))
 
 
-def fixed(arrays):
-    return pl.BlockSpec((16, arrays, ROWS, 128), lambda j: (0, 0, 0, 0))
-
-
 def probs(half, qk):
     return pl.pallas_call(
         probs_kernel,
         out_shape=jax.ShapeDtypeStruct((8, 1024, 1024), BF),
         grid=(8,),
-        in_specs=[SCALAR, fixed(2)],
+        in_specs=[SCALAR, VMEM],
         out_specs=EACH_HEAD,
         scratch_shapes=[TILES, TILES, WINDOW],
-        compiler_params=pltpu.CompilerParams(vmem_limit_bytes=VMEM_LIMIT),
+        compiler_params=pltpu.CompilerParams(vmem_limit_bytes=44 * 1024 * 1024),
         cost_estimate=pl.CostEstimate(
             flops=20_000_000_000, bytes_accessed=20_000_000, transcendentals=8_400_000
         ),
@@ -312,10 +308,10 @@
         grads_kernel,
         out_shape=jax.ShapeDtypeStruct((16, 3, ROWS, 128), BF),
         grid=(8,),
-        in_specs=[SCALAR, fixed(2), fixed(2), EACH_HEAD],
-        out_specs=fixed(3),
+        in_specs=[SCALAR, VMEM, VMEM, EACH_HEAD],
+        out_specs=VMEM,
         scratch_shapes=[TILES] * 7 + [WINDOW, WINDOW, pltpu.VMEM((1024, 1024), BF)],
-        compiler_params=pltpu.CompilerParams(vmem_limit_bytes=VMEM_LIMIT),
+        compiler_params=pltpu.CompilerParams(vmem_limit_bytes=44 * 1024 * 1024),
         cost_estimate=pl.CostEstimate(
             flops=25_000_000_000, bytes_accessed=26_000_000, transcendentals=0
         ),

time: 256 us -> 254 us (level)
  Pallas kernels: 80.7 us -> 74.9 us
  transfers between devices with their start and end apart: 2 -> 2, of which waited for: 2 -> 2; matrix products, arithmetic and copies ran while one was open for 0% -> 0% of each run, Pallas kernels for 18% -> 17%
where the time goes in v5:
time: 254 us; the launch traced here: 253 us
  blocking collectives  131 us (52%)
  Pallas kernels  74.9 us (29%)
  waiting for transfers between devices  19.7 us (8%)
  starting transfers between devices  19.2 us (8%)
  local copies, waits for them, and re-layouts  7.04 us (3%)
    all_to_all x3, blocking collectives, exchange(): return lax.all_to_all(x, axis, 0, 0, tiled=True)  131 us
    pallas_call x1, Pallas kernels, temporal(): pl.pallas_call(temporal_kernel, out_shape=jax.ShapeDtypeStruct((8, 64, D)...  25.6 us
    pallas_call x1, Pallas kernels, grads(): pl.pallas_call(grads_kernel, out_shape=jax.ShapeDtypeStruct((16, 3, ROWS,...  24.8 us
    all_to_all x2, waiting for transfers between devices, exchange(): return lax.all_to_all(x, axis, 0, 0, tiled=True)  19.7 us
    all_to_all x2, starting transfers between devices, exchange(): return lax.all_to_all(x, axis, 0, 0, tiled=True)  19.2 us
    pallas_call x1, Pallas kernels, probs(): pl.pallas_call(probs_kernel, out_shape=jax.ShapeDtypeStruct((8, 1024, 102...  18 us
    unnamed x18, local copies, waits for them, and re-layouts  7.04 us
  transfers between devices with their start and end apart: 2, of which 2 were waited for; matrix products, arithmetic and copies ran while one was open for 0% of the time, Pallas kernels for 17%

profile of v5, /device:TPU:1, one launch (start us, length us, event | category | flops | bytes accessed | tf_op | source)
XLA Modules:
  0.0 253.5 jit_solution(15064340701880734402)
XLA Ops:
  0.6 0.0 copy-start.1
  0.6 1.3 copy-done.1
  1.9 0.0 copy-start.2
  1.9 1.3 copy-done.2
  3.2 0.0 copy-start.5
  3.2 0.0 copy-start.6
  3.2 0.0 copy-start.7
  3.2 0.0 copy-start.8
  3.2 1.8 pack.1
  5.0 0.0 copy-done.5
  5.0 0.5 copy-done.6
  5.6 0.4 copy-done.7
  6.0 0.4 copy-done.8
  6.4 0.7 copy_bitcast_fusion
  7.1 59.9 %all_to_all.25.r_ref = bf16[8,4,64,1152]{3,2,1,0:T(8,128)(2,1)} all-to-all(bf16[8,4,64,1152]{3,2,1,0:T(8,128)(2,1)S(1)} %copy_bitcast_fusion), channel_id=1, replica_groups=mesh['tm'=8,'space'=16] {'tm'}, dimensions={0} | all-to-all | bytes 9437184 | tf_op jit(solution)/shard_map/all_to_all | solution.py:349
  66.9 9.8 %all-to-all-start.1 = ((bf16[16,2,288,128]{3,2,1,0:T(8,128)(2,1)}), bf16[16,2,288,128]{3,2,1,0:T(8,128)(2,1)S(1)}, u32[]{:S(2)}, u32[]{:S(2)}) async-start(bf16[16,2,288,128]{3,2,1,0:T(8,128)(2,1)} %bitcast.7), calls=%async_computation.1 | async-start | bytes 4718592 | tf_op jit(solution)/shard_map/all_to_all | solution.py:349
  76.8 25.6 %temporal.1 = bf16[8,64,1152]{2,1,0:T(8,128)(2,1)} custom-call(bf16[8,4,64,1152]{3,2,1,0:T(8,128)(2,1)} %all_to_all.25.r_ref, bf16[1152,1152]{1,0:T(8,128)(2,1)} %wo_hbm.1, bf16[1152,1152]{1,0:T(8,128)(2,1)} %wq_hbm.1, bf16[1152,1152]{1,0:T(8,128)(2,1)} %wk_hbm.1, bf16[1152,1152]{1,0:T(8,128)(2,1)} %wv_hbm.1), custom_call_target="tpu_custom_call" | custom-call | flops 20000000000 | bytes 16000000 | tf_op jit(solution)/shard_map/temporal/pallas_call | solution.py:110
  102.4 0.0 copy-start.4
  102.4 6.0 %all-to-all-done.1.qk_ref = bf16[16,2,288,128]{3,2,1,0:T(8,128)(2,1)S(1)} async-done(((bf16[16,2,288,128]{3,2,1,0:T(8,128)(2,1)}), bf16[16,2,288,128]{3,2,1,0:T(8,128)(2,1)S(1)}, u32[]{:S(2)}, u32[]{:S(2)}) %all-to-all-start.1) | async-done | bytes 2359328 | tf_op jit(solution)/shard_map/all_to_all | solution.py:349
  108.4 20.0 %all_to_all.26.m_ref = bf16[8,64,1152]{2,1,0:T(8,128)(2,1)S(1)} all-to-all(bf16[8,64,1152]{2,1,0:T(8,128)(2,1)} %temporal.1), channel_id=1, replica_groups=mesh['tm'=8,'space'=16] {'tm'}, dimensions={0} | all-to-all | bytes 2359296 | tf_op jit(solution)/shard_map/all_to_all | solution.py:349
  128.3 0.0 copy-done.4
  128.4 0.0 copy-start.3
  128.4 1.7 copy-done.3
  130.1 2.6 %project.1 = (bf16[8,64,1152]{2,1,0:T(8,128)(2,1)}, bf16[8,2,2,288,128]{4,3,2,1,0:T(8,128)(2,1)S(1)}) custom-call(bf16[8,64,1152]{2,1,0:T(8,128)(2,1)S(1)} %all_to_all.26.m_ref, bf16[1152,1152]{1,0:T(8,128)(2,1)S(1)} %copy-done.3, bf16[8,64,1152]{2,1,0:T(8,128)(2,1)S(1)} %copy-done.4), custom_call_target="tpu_custom_call" | custom-call | flops 4000000000 | bytes 8000000 | tf_op jit(solution)/shard_map/project/pallas_call | solution.py:184
  132.7 0.0 copy-start
  132.7 1.4 copy-done
  134.1 9.4 %all-to-all-start.3 = ((bf16[16,2,288,128]{3,2,1,0:T(8,128)(2,1)}), bf16[16,2,288,128]{3,2,1,0:T(8,128)(2,1)}, u32[]{:S(2)}, u32[]{:S(2)}) async-start(bf16[16,2,288,128]{3,2,1,0:T(8,128)(2,1)} %bitcast.13), calls=%async_computation.3 | async-start | bytes 4718592 | tf_op jit(solution)/shard_map/all_to_all | solution.py:349
  143.5 18.0 %probs.1.p_ref = bf16[8,1024,1024]{2,1,0:T(8,128)(2,1)} custom-call(s32[1]{0:T(128)} %bitcast.half_ref, bf16[16,2,288,128]{3,2,1,0:T(8,128)(2,1)S(1)} %all-to-all-done.1.qk_ref), custom_call_target="tpu_custom_call" | custom-call | flops 20000000000 | bytes 20000000 | tf_op jit(solution)/shard_map/probs/pallas_call | solution.py:261
  161.5 13.7 %all-to-all-done.3.vg_ref = bf16[16,2,288,128]{3,2,1,0:T(8,128)(2,1)} async-done(((bf16[16,2,288,128]{3,2,1,0:T(8,128)(2,1)}), bf16[16,2,288,128]{3,2,1,0:T(8,128)(2,1)}, u32[]{:S(2)}, u32[]{:S(2)}) %all-to-all-start.3) | async-done | bytes 2359328 | tf_op jit(solution)/shard_map/all_to_all | solution.py:349
  175.2 24.8 %grads.1 = bf16[16,3,288,128]{3,2,1,0:T(8,128)(2,1)S(1)} custom-call(s32[1]{0:T(128)} %bitcast.half_ref, bf16[16,2,288,128]{3,2,1,0:T(8,128)(2,1)S(1)} %all-to-all-done.1.qk_ref, bf16[16,2,288,128]{3,2,1,0:T(8,128)(2,1)} %all-to-all-done.3.vg_ref, bf16[8,1024,1024]{2,1,0:T(8,128)(2,1)} %probs.1.p_ref), custom_call_target="tpu_custom_call" | custom-call | flops 24999999488 | bytes 26000000 | tf_op jit(solution)/shard_map/grads/pallas_call | solution.py:307
  200.0 51.4 %all_to_all.27 = bf16[16,3,288,128]{3,2,1,0:T(8,128)(2,1)S(1)} all-to-all(bf16[16,3,288,128]{3,2,1,0:T(8,128)(2,1)S(1)} %grads.1), channel_id=1, replica_groups=mesh['tm'=8,'space'=16] {'space'}, dimensions={0} | all-to-all | bytes 7077888 | tf_op jit(solution)/shard_map/all_to_all | solution.py:349
  251.4 2.0 unpack.1
Async XLA Ops:
  0.6 1.3 copy-start.1
  1.9 1.3 copy-start.2
  3.2 1.8 copy-start.5
  3.2 2.4 copy-start.6
  3.2 2.8 %copy-start.7 = (bf16[8,64,1152]{2,1,0:T(8,128)(2,1)S(1)}, bf16[8,64,1152]{2,1,0:T(8,128)(2,1)}, u32[]{:S(2)}) copy-start(bf16[8,64,1152]{2,1,0:T(8,128)(2,1)} %param.13) | copy-start | bytes 3538948
  3.2 3.2 %copy-start.8 = (bf16[8,64,1152]{2,1,0:T(8,128)(2,1)S(1)}, bf16[8,64,1152]{2,1,0:T(8,128)(2,1)}, u32[]{:S(2)}) copy-start(bf16[8,64,1152]{2,1,0:T(8,128)(2,1)} %param.12) | copy-start | bytes 3538948
  66.9 41.4 %all-to-all-start.1 = ((bf16[16,2,288,128]{3,2,1,0:T(8,128)(2,1)}), bf16[16,2,288,128]{3,2,1,0:T(8,128)(2,1)S(1)}, u32[]{:S(2)}, u32[]{:S(2)}) async-start(bf16[16,2,288,128]{3,2,1,0:T(8,128)(2,1)} %bitcast.7), calls=%async_computation.1 | async-start | bytes 4718592 | tf_op jit(solution)/shard_map/all_to_all | solution.py:349
  102.4 25.9 %copy-start.4 = (bf16[8,64,1152]{2,1,0:T(8,128)(2,1)S(1)}, bf16[8,64,1152]{2,1,0:T(8,128)(2,1)}, u32[]{:S(2)}) copy-start(bf16[8,64,1152]{2,1,0:T(8,128)(2,1)} %v_ref.1) | copy-start | bytes 3538948
  128.4 1.8 copy-start.3
  132.7 1.4 copy-start
  134.1 41.1 %all-to-all-start.3 = ((bf16[16,2,288,128]{3,2,1,0:T(8,128)(2,1)}), bf16[16,2,288,128]{3,2,1,0:T(8,128)(2,1)}, u32[]{:S(2)}, u32[]{:S(2)}) async-start(bf16[16,2,288,128]{3,2,1,0:T(8,128)(2,1)} %bitcast.13), calls=%async_computation.3 | async-start | bytes 4718592 | tf_op jit(solution)/shard_map/all_to_all | solution.py:349

commit v6 on v5

--- a/solution.py
+++ b/solution.py
@@ -113,7 +113,7 @@
         in_specs=[vmem, hbm, hbm, hbm, hbm],
         out_specs=vmem,
         scratch_shapes=[weight] * 4 + [rows] * 8 + [pltpu.SemaphoreType.DMA((4,))],
-        compiler_params=pltpu.CompilerParams(vmem_limit_bytes=VMEM_LIMIT),
+        compiler_params=pltpu.CompilerParams(vmem_limit_bytes=50 * 1024 * 1024),
         cost_estimate=pl.CostEstimate(
             flops=20_000_000_000, bytes_accessed=16_000_000, transcendentals=2_000_000
         ),

time: 254 us -> 253 us (level)
    unnamed x18 -> x20, local copies, waits for them, and re-layouts: 7.04 us -> 8.8 us
where the time goes in v6:
time: 253 us
  blocking collectives  130 us (51%)
  Pallas kernels  74.1 us (29%)
  starting transfers between devices  20 us (8%)
  waiting for transfers between devices  18.7 us (7%)
  local copies, waits for them, and re-layouts  8.8 us (3%)
    all_to_all x3, blocking collectives, exchange(): return lax.all_to_all(x, axis, 0, 0, tiled=True)  130 us
    pallas_call x1, Pallas kernels, temporal(): pl.pallas_call(temporal_kernel, out_shape=jax.ShapeDtypeStruct((8, 64, D)...  24.8 us
    pallas_call x1, Pallas kernels, grads(): pl.pallas_call(grads_kernel, out_shape=jax.ShapeDtypeStruct((16, 3, ROWS,...  24.8 us
    all_to_all x2, starting transfers between devices, exchange(): return lax.all_to_all(x, axis, 0, 0, tiled=True)  20 us
    all_to_all x2, waiting for transfers between devices, exchange(): return lax.all_to_all(x, axis, 0, 0, tiled=True)  18.7 us
    pallas_call x1, Pallas kernels, probs(): pl.pallas_call(probs_kernel, out_shape=jax.ShapeDtypeStruct((8, 1024, 102...  18 us
    unnamed x20, local copies, waits for them, and re-layouts  8.8 us
  transfers between devices with their start and end apart: 2, of which 2 were waited for; matrix products, arithmetic and copies ran while one was open for 0% of the time, Pallas kernels for 17%

profile of v6, /device:TPU:1, one launch (start us, length us, event | category | flops | bytes accessed | tf_op | source)
XLA Modules:
  0.0 252.5 jit_solution(3876197177319002521)
XLA Ops:
  0.6 0.0 copy-start.1
  0.6 1.3 copy-done.1
  1.9 0.0 copy-start.2
  1.9 1.3 copy-done.2
  3.2 0.0 copy-start.6
  3.2 0.0 copy-start.7
  3.2 0.0 copy-start.8
  3.2 0.0 copy-start.9
  3.2 1.8 pack.1
  5.0 0.0 copy-done.6
  5.0 0.5 copy-done.7
  5.6 0.4 copy-done.8
  6.0 0.4 copy-done.9
  6.4 0.7 copy_bitcast_fusion
  7.1 59.9 %all_to_all.25.r_ref = bf16[8,4,64,1152]{3,2,1,0:T(8,128)(2,1)} all-to-all(bf16[8,4,64,1152]{3,2,1,0:T(8,128)(2,1)S(1)} %copy_bitcast_fusion), channel_id=1, replica_groups=mesh['tm'=8,'space'=16] {'tm'}, dimensions={0} | all-to-all | bytes 9437184 | tf_op jit(solution)/shard_map/all_to_all | solution.py:349
  66.9 9.8 %all-to-all-start.1 = ((bf16[16,2,288,128]{3,2,1,0:T(8,128)(2,1)}), bf16[16,2,288,128]{3,2,1,0:T(8,128)(2,1)S(1)}, u32[]{:S(2)}, u32[]{:S(2)}) async-start(bf16[16,2,288,128]{3,2,1,0:T(8,128)(2,1)} %bitcast.7), calls=%async_computation.1 | async-start | bytes 4718592 | tf_op jit(solution)/shard_map/all_to_all | solution.py:349
  76.8 0.0 copy-start.3
  76.8 1.7 copy-done.3
  78.5 24.8 %temporal.1 = bf16[8,64,1152]{2,1,0:T(8,128)(2,1)S(1)} custom-call(bf16[8,4,64,1152]{3,2,1,0:T(8,128)(2,1)} %all_to_all.25.r_ref, bf16[1152,1152]{1,0:T(8,128)(2,1)S(1)} %copy-done.3, bf16[1152,1152]{1,0:T(8,128)(2,1)} %wq_hbm.1, bf16[1152,1152]{1,0:T(8,128)(2,1)} %wk_hbm.1, bf16[1152,1152]{1,0:T(8,128)(2,1)} %wv_hbm.1), custom_call_target="tpu_custom_call" | custom-call | flops 20000000000 | bytes 16000000 | tf_op jit(solution)/shard_map/temporal/pallas_call | solution.py:110
  103.4 5.0 %all-to-all-done.1.qk_ref = bf16[16,2,288,128]{3,2,1,0:T(8,128)(2,1)S(1)} async-done(((bf16[16,2,288,128]{3,2,1,0:T(8,128)(2,1)}), bf16[16,2,288,128]{3,2,1,0:T(8,128)(2,1)S(1)}, u32[]{:S(2)}, u32[]{:S(2)}) %all-to-all-start.1) | async-done | bytes 2359328 | tf_op jit(solution)/shard_map/all_to_all | solution.py:349
  108.4 0.0 copy-start.5
  108.4 18.2 %all_to_all.26.m_ref = bf16[8,64,1152]{2,1,0:T(8,128)(2,1)S(1)} all-to-all(bf16[8,64,1152]{2,1,0:T(8,128)(2,1)S(1)} %temporal.1), channel_id=1, replica_groups=mesh['tm'=8,'space'=16] {'tm'}, dimensions={0} | all-to-all | bytes 2359296 | tf_op jit(solution)/shard_map/all_to_all | solution.py:349
  126.6 0.0 copy-done.5
  126.6 0.0 copy-start.4
  126.6 1.7 copy-done.4
  128.4 2.6 %project.1 = (bf16[8,64,1152]{2,1,0:T(8,128)(2,1)}, bf16[8,2,2,288,128]{4,3,2,1,0:T(8,128)(2,1)S(1)}) custom-call(bf16[8,64,1152]{2,1,0:T(8,128)(2,1)S(1)} %all_to_all.26.m_ref, bf16[1152,1152]{1,0:T(8,128)(2,1)S(1)} %copy-done.4, bf16[8,64,1152]{2,1,0:T(8,128)(2,1)S(1)} %copy-done.5), custom_call_target="tpu_custom_call" | custom-call | flops 4000000000 | bytes 8000000 | tf_op jit(solution)/shard_map/project/pallas_call | solution.py:184
  131.0 0.0 copy-start
  131.0 1.4 copy-done
  132.4 10.1 %all-to-all-start.3 = ((bf16[16,2,288,128]{3,2,1,0:T(8,128)(2,1)}), bf16[16,2,288,128]{3,2,1,0:T(8,128)(2,1)}, u32[]{:S(2)}, u32[]{:S(2)}) async-start(bf16[16,2,288,128]{3,2,1,0:T(8,128)(2,1)} %bitcast.13), calls=%async_computation.3 | async-start | bytes 4718592 | tf_op jit(solution)/shard_map/all_to_all | solution.py:349
  142.6 18.0 %probs.1.p_ref = bf16[8,1024,1024]{2,1,0:T(8,128)(2,1)} custom-call(s32[1]{0:T(128)} %bitcast.half_ref, bf16[16,2,288,128]{3,2,1,0:T(8,128)(2,1)S(1)} %all-to-all-done.1.qk_ref), custom_call_target="tpu_custom_call" | custom-call | flops 20000000000 | bytes 20000000 | tf_op jit(solution)/shard_map/probs/pallas_call | solution.py:261
  160.6 13.7 %all-to-all-done.3.vg_ref = bf16[16,2,288,128]{3,2,1,0:T(8,128)(2,1)} async-done(((bf16[16,2,288,128]{3,2,1,0:T(8,128)(2,1)}), bf16[16,2,288,128]{3,2,1,0:T(8,128)(2,1)}, u32[]{:S(2)}, u32[]{:S(2)}) %all-to-all-start.3) | async-done | bytes 2359328 | tf_op jit(solution)/shard_map/all_to_all | solution.py:349
  174.3 24.8 %grads.1 = bf16[16,3,288,128]{3,2,1,0:T(8,128)(2,1)S(1)} custom-call(s32[1]{0:T(128)} %bitcast.half_ref, bf16[16,2,288,128]{3,2,1,0:T(8,128)(2,1)S(1)} %all-to-all-done.1.qk_ref, bf16[16,2,288,128]{3,2,1,0:T(8,128)(2,1)} %all-to-all-done.3.vg_ref, bf16[8,1024,1024]{2,1,0:T(8,128)(2,1)} %probs.1.p_ref), custom_call_target="tpu_custom_call" | custom-call | flops 24999999488 | bytes 26000000 | tf_op jit(solution)/shard_map/grads/pallas_call | solution.py:307
  199.1 51.4 %all_to_all.27 = bf16[16,3,288,128]{3,2,1,0:T(8,128)(2,1)S(1)} all-to-all(bf16[16,3,288,128]{3,2,1,0:T(8,128)(2,1)S(1)} %grads.1), channel_id=1, replica_groups=mesh['tm'=8,'space'=16] {'space'}, dimensions={0} | all-to-all | bytes 7077888 | tf_op jit(solution)/shard_map/all_to_all | solution.py:349
  250.5 2.0 unpack.1
Async XLA Ops:
  0.6 1.3 copy-start.1
  1.9 1.3 copy-start.2
  3.2 1.8 copy-start.6
  3.2 2.4 copy-start.7
  3.2 2.8 %copy-start.8 = (bf16[8,64,1152]{2,1,0:T(8,128)(2,1)S(1)}, bf16[8,64,1152]{2,1,0:T(8,128)(2,1)}, u32[]{:S(2)}) copy-start(bf16[8,64,1152]{2,1,0:T(8,128)(2,1)} %param.13) | copy-start | bytes 3538948
  3.2 3.2 %copy-start.9 = (bf16[8,64,1152]{2,1,0:T(8,128)(2,1)S(1)}, bf16[8,64,1152]{2,1,0:T(8,128)(2,1)}, u32[]{:S(2)}) copy-start(bf16[8,64,1152]{2,1,0:T(8,128)(2,1)} %param.12) | copy-start | bytes 3538948
  66.9 41.4 %all-to-all-start.1 = ((bf16[16,2,288,128]{3,2,1,0:T(8,128)(2,1)}), bf16[16,2,288,128]{3,2,1,0:T(8,128)(2,1)S(1)}, u32[]{:S(2)}, u32[]{:S(2)}) async-start(bf16[16,2,288,128]{3,2,1,0:T(8,128)(2,1)} %bitcast.7), calls=%async_computation.1 | async-start | bytes 4718592 | tf_op jit(solution)/shard_map/all_to_all | solution.py:349
  76.8 1.7 copy-start.3
  108.4 18.3 %copy-start.5 = (bf16[8,64,1152]{2,1,0:T(8,128)(2,1)S(1)}, bf16[8,64,1152]{2,1,0:T(8,128)(2,1)}, u32[]{:S(2)}) copy-start(bf16[8,64,1152]{2,1,0:T(8,128)(2,1)} %v_ref.1) | copy-start | bytes 3538948
  126.6 1.8 copy-start.4
  131.0 1.4 copy-start
  132.4 41.9 %all-to-all-start.3 = ((bf16[16,2,288,128]{3,2,1,0:T(8,128)(2,1)}), bf16[16,2,288,128]{3,2,1,0:T(8,128)(2,1)}, u32[]{:S(2)}, u32[]{:S(2)}) async-start(bf16[16,2,288,128]{3,2,1,0:T(8,128)(2,1)} %bitcast.13), calls=%async_computation.3 | async-start | bytes 4718592 | tf_op jit(solution)/shard_map/all_to_all | solution.py:349

commit v7 on v6

--- a/solution.py
+++ b/solution.py
@@ -156,7 +156,7 @@
         out_shape=jax.ShapeDtypeStruct((8, 2, len(arrays), ROWS, 128), BF),
         in_specs=[vmem] * len(arrays),
         out_specs=vmem,
-        compiler_params=pltpu.CompilerParams(vmem_limit_bytes=32 * 1024 * 1024),
+        compiler_params=pltpu.CompilerParams(vmem_limit_bytes=60 * 1024 * 1024),
         name="pack",
     )(*arrays)
 

time: 253 us -> 252 us (level)
  local copies, waits for them, and re-layouts: 8.8 us -> 4.9 us
    unnamed x20 -> x14, local copies, waits for them, and re-layouts: 8.8 us -> 4.9 us
where the time goes in v7:
time: 252 us
  blocking collectives  130 us (52%)
  Pallas kernels  75.9 us (30%)
  starting transfers between devices  20 us (8%)
  waiting for transfers between devices  18.7 us (7%)
  local copies, waits for them, and re-layouts  4.9 us (2%)
    all_to_all x3, blocking collectives, exchange(): return lax.all_to_all(x, axis, 0, 0, tiled=True)  130 us
    pallas_call x1, Pallas kernels, temporal(): pl.pallas_call(temporal_kernel, out_shape=jax.ShapeDtypeStruct((8, 64, D)...  24.8 us
    pallas_call x1, Pallas kernels, grads(): pl.pallas_call(grads_kernel, out_shape=jax.ShapeDtypeStruct((16, 3, ROWS,...  24.8 us
    all_to_all x2, starting transfers between devices, exchange(): return lax.all_to_all(x, axis, 0, 0, tiled=True)  20 us
    all_to_all x2, waiting for transfers between devices, exchange(): return lax.all_to_all(x, axis, 0, 0, tiled=True)  18.7 us
    pallas_call x1, Pallas kernels, probs(): pl.pallas_call(probs_kernel, out_shape=jax.ShapeDtypeStruct((8, 1024, 102...  18 us
  transfers between devices with their start and end apart: 2, of which 2 were waited for; matrix products, arithmetic and copies ran while one was open for 0% of the time, Pallas kernels for 17%

profile of v7, /device:TPU:1, one launch (start us, length us, event | category | flops | bytes accessed | tf_op | source)
XLA Modules:
  0.0 251.5 jit_solution(12142745570774438900)
XLA Ops:
  0.6 0.0 copy-start.4
  0.6 0.0 copy-start.5
  0.7 0.0 copy-start.6
  0.7 3.6 %pack.1 = bf16[8,2,2,288,128]{4,3,2,1,0:T(8,128)(2,1)} custom-call(bf16[8,64,1152]{2,1,0:T(8,128)(2,1)} %refs_0_.1, bf16[8,64,1152]{2,1,0:T(8,128)(2,1)} %refs_1_.1), custom_call_target="tpu_custom_call" | custom-call | tf_op jit(solution)/shard_map/pack/pallas_call | solution.py:154
  4.3 0.0 copy-done.4
  4.3 0.0 copy-done.5
  4.3 0.0 copy-done.6
  4.3 1.8 copy_bitcast_fusion
  6.1 59.9 %all_to_all.25.r_ref = bf16[8,4,64,1152]{3,2,1,0:T(8,128)(2,1)} all-to-all(bf16[8,4,64,1152]{3,2,1,0:T(8,128)(2,1)S(1)} %copy_bitcast_fusion), channel_id=1, replica_groups=mesh['tm'=8,'space'=16] {'tm'}, dimensions={0} | all-to-all | bytes 9437184 | tf_op jit(solution)/shard_map/all_to_all | solution.py:349
  65.9 9.8 %all-to-all-start.1 = ((bf16[16,2,288,128]{3,2,1,0:T(8,128)(2,1)}), bf16[16,2,288,128]{3,2,1,0:T(8,128)(2,1)S(1)}, u32[]{:S(2)}, u32[]{:S(2)}) async-start(bf16[16,2,288,128]{3,2,1,0:T(8,128)(2,1)} %bitcast.14), calls=%async_computation.1 | async-start | bytes 4718592 | tf_op jit(solution)/shard_map/all_to_all | solution.py:349
  75.8 0.0 copy-start.1
  75.8 1.7 copy-done.1
  77.5 24.8 %temporal.1 = bf16[8,64,1152]{2,1,0:T(8,128)(2,1)S(1)} custom-call(bf16[8,4,64,1152]{3,2,1,0:T(8,128)(2,1)} %all_to_all.25.r_ref, bf16[1152,1152]{1,0:T(8,128)(2,1)S(1)} %copy-done.1, bf16[1152,1152]{1,0:T(8,128)(2,1)} %wq_hbm.1, bf16[1152,1152]{1,0:T(8,128)(2,1)} %wk_hbm.1, bf16[1152,1152]{1,0:T(8,128)(2,1)} %wv_hbm.1), custom_call_target="tpu_custom_call" | custom-call | flops 20000000000 | bytes 16000000 | tf_op jit(solution)/shard_map/temporal/pallas_call | solution.py:110
  102.4 5.0 %all-to-all-done.1.qk_ref = bf16[16,2,288,128]{3,2,1,0:T(8,128)(2,1)S(1)} async-done(((bf16[16,2,288,128]{3,2,1,0:T(8,128)(2,1)}), bf16[16,2,288,128]{3,2,1,0:T(8,128)(2,1)S(1)}, u32[]{:S(2)}, u32[]{:S(2)}) %all-to-all-start.1) | async-done | bytes 2359328 | tf_op jit(solution)/shard_map/all_to_all | solution.py:349
  107.4 0.0 copy-start.3
  107.4 18.2 %all_to_all.26.m_ref = bf16[8,64,1152]{2,1,0:T(8,128)(2,1)S(1)} all-to-all(bf16[8,64,1152]{2,1,0:T(8,128)(2,1)S(1)} %temporal.1), channel_id=1, replica_groups=mesh['tm'=8,'space'=16] {'tm'}, dimensions={0} | all-to-all | bytes 2359296 | tf_op jit(solution)/shard_map/all_to_all | solution.py:349
  125.6 0.0 copy-done.3
  125.6 0.0 copy-start.2
  125.6 1.7 copy-done.2
  127.4 2.6 %project.1 = (bf16[8,64,1152]{2,1,0:T(8,128)(2,1)}, bf16[8,2,2,288,128]{4,3,2,1,0:T(8,128)(2,1)S(1)}) custom-call(bf16[8,64,1152]{2,1,0:T(8,128)(2,1)S(1)} %all_to_all.26.m_ref, bf16[1152,1152]{1,0:T(8,128)(2,1)S(1)} %copy-done.2, bf16[8,64,1152]{2,1,0:T(8,128)(2,1)S(1)} %copy-done.3), custom_call_target="tpu_custom_call" | custom-call | flops 4000000000 | bytes 8000000 | tf_op jit(solution)/shard_map/project/pallas_call | solution.py:184
  130.0 0.0 copy-start
  130.0 1.4 copy-done
  131.4 10.1 %all-to-all-start.3 = ((bf16[16,2,288,128]{3,2,1,0:T(8,128)(2,1)}), bf16[16,2,288,128]{3,2,1,0:T(8,128)(2,1)}, u32[]{:S(2)}, u32[]{:S(2)}) async-start(bf16[16,2,288,128]{3,2,1,0:T(8,128)(2,1)} %bitcast.13), calls=%async_computation.3 | async-start | bytes 4718592 | tf_op jit(solution)/shard_map/all_to_all | solution.py:349
  141.6 18.0 %probs.1.p_ref = bf16[8,1024,1024]{2,1,0:T(8,128)(2,1)} custom-call(s32[1]{0:T(128)} %bitcast.half_ref, bf16[16,2,288,128]{3,2,1,0:T(8,128)(2,1)S(1)} %all-to-all-done.1.qk_ref), custom_call_target="tpu_custom_call" | custom-call | flops 20000000000 | bytes 20000000 | tf_op jit(solution)/shard_map/probs/pallas_call | solution.py:261
  159.6 13.7 %all-to-all-done.3.vg_ref = bf16[16,2,288,128]{3,2,1,0:T(8,128)(2,1)} async-done(((bf16[16,2,288,128]{3,2,1,0:T(8,128)(2,1)}), bf16[16,2,288,128]{3,2,1,0:T(8,128)(2,1)}, u32[]{:S(2)}, u32[]{:S(2)}) %all-to-all-start.3) | async-done | bytes 2359328 | tf_op jit(solution)/shard_map/all_to_all | solution.py:349
  173.3 24.8 %grads.1 = bf16[16,3,288,128]{3,2,1,0:T(8,128)(2,1)S(1)} custom-call(s32[1]{0:T(128)} %bitcast.half_ref, bf16[16,2,288,128]{3,2,1,0:T(8,128)(2,1)S(1)} %all-to-all-done.1.qk_ref, bf16[16,2,288,128]{3,2,1,0:T(8,128)(2,1)} %all-to-all-done.3.vg_ref, bf16[8,1024,1024]{2,1,0:T(8,128)(2,1)} %probs.1.p_ref), custom_call_target="tpu_custom_call" | custom-call | flops 24999999488 | bytes 26000000 | tf_op jit(solution)/shard_map/grads/pallas_call | solution.py:307
  198.1 51.4 %all_to_all.27 = bf16[16,3,288,128]{3,2,1,0:T(8,128)(2,1)S(1)} all-to-all(bf16[16,3,288,128]{3,2,1,0:T(8,128)(2,1)S(1)} %grads.1), channel_id=1, replica_groups=mesh['tm'=8,'space'=16] {'space'}, dimensions={0} | all-to-all | bytes 7077888 | tf_op jit(solution)/shard_map/all_to_all | solution.py:349
  249.5 2.0 unpack.1
Async XLA Ops:
  0.6 3.6 %copy-start.4 = (bf16[8,64,1152]{2,1,0:T(8,128)(2,1)S(1)}, bf16[8,64,1152]{2,1,0:T(8,128)(2,1)}, u32[]{:S(2)}) copy-start(bf16[8,64,1152]{2,1,0:T(8,128)(2,1)} %param.18) | copy-start | bytes 3538948
  0.6 3.6 %copy-start.5 = (bf16[8,64,1152]{2,1,0:T(8,128)(2,1)S(1)}, bf16[8,64,1152]{2,1,0:T(8,128)(2,1)}, u32[]{:S(2)}) copy-start(bf16[8,64,1152]{2,1,0:T(8,128)(2,1)} %param.14) | copy-start | bytes 3538948
  0.7 3.6 %copy-start.6 = (bf16[8,64,1152]{2,1,0:T(8,128)(2,1)S(1)}, bf16[8,64,1152]{2,1,0:T(8,128)(2,1)}, u32[]{:S(2)}) copy-start(bf16[8,64,1152]{2,1,0:T(8,128)(2,1)} %param.13) | copy-start | bytes 3538948
  65.9 41.4 %all-to-all-start.1 = ((bf16[16,2,288,128]{3,2,1,0:T(8,128)(2,1)}), bf16[16,2,288,128]{3,2,1,0:T(8,128)(2,1)S(1)}, u32[]{:S(2)}, u32[]{:S(2)}) async-start(bf16[16,2,288,128]{3,2,1,0:T(8,128)(2,1)} %bitcast.14), calls=%async_computation.1 | async-start | bytes 4718592 | tf_op jit(solution)/shard_map/all_to_all | solution.py:349
  75.8 1.7 copy-start.1
  107.4 18.3 %copy-start.3 = (bf16[8,64,1152]{2,1,0:T(8,128)(2,1)S(1)}, bf16[8,64,1152]{2,1,0:T(8,128)(2,1)}, u32[]{:S(2)}) copy-start(bf16[8,64,1152]{2,1,0:T(8,128)(2,1)} %v_ref.1) | copy-start | bytes 3538948
  125.6 1.8 copy-start.2
  130.0 1.4 copy-start
  131.4 41.9 %all-to-all-start.3 = ((bf16[16,2,288,128]{3,2,1,0:T(8,128)(2,1)}), bf16[16,2,288,128]{3,2,1,0:T(8,128)(2,1)}, u32[]{:S(2)}, u32[]{:S(2)}) async-start(bf16[16,2,288,128]{3,2,1,0:T(8,128)(2,1)} %bitcast.13), calls=%async_computation.3 | async-start | bytes 4718592 | tf_op jit(solution)/shard_map/all_to_all | solution.py:349
